TPU v7x, 32 devices: a whole 2x2x4 slice. The times are simulated.
32 devices in a mesh: slab: 4 (over z), blk: 8 (over y, x, core).
Axes of the slice: x: 2, y: 2, z: 4, core: 2. Of those that a mesh axis runs over, the one named last changes fastest.
Arguments:
- fixed_image: bfloat16 [256, 128, 128], P('blk', 'slab'), may hold values from -6 to 6
- moving_image: bfloat16 [256, 128, 128], P('blk', 'slab'), may hold values from -6 to 6
- fetch_owner: int32 [8, 4, 4, 4], P('blk', 'slab'), may hold values from 0 to 7, as said below
- fetch_block: int32 [8, 4, 4, 4], P('blk', 'slab'), may hold values from 0 to 3
- fetch_count: int32 [8, 4, 4], P('blk', 'slab'), may hold values from 1 to 4, as said below
- interp_level: int32 [8, 4, 4, 3, 4], P('blk', 'slab'), may hold values from 0 to 7
- block_mask: int32 [8, 4, 4], P('blk', 'slab'), may hold values 0 or 1
Outputs:
- update: float32 [3, 256, 128, 128], P(None, 'blk', 'slab')
Inputs may be any that keep to these rules, and one draw needn't show every extreme that they name: `fetch_owner`: entries k < fetch_count of one device's lists name any one owner at most 2 times in all; in every draw some owner is named exactly 2 times by every device of its slab. Entries k >= fetch_count are not read. `fetch_count`: every device has a block whose list holds 4 entries.
All inputs are finite; a program needn't handle non-finite values. No bound on the sum of `block_mask` on one device may be relied on, other than what follows from the above.
Results may differ from a plain program's by a relative error of at most 0.006.
Values may be sent and summed in bfloat16 or wider, within the bound.
A program may use at most 64 MiB of HBM per device.

v0:
```python
import math

import jax
import jax.numpy as jnp
from jax import lax
from jax.sharding import PartitionSpec as P

LEVELS = 8
BOX_RADIUS = 2
SMOOTH_RADIUS = 3


sigma_smooth = 1.5
step_length = 2.0
var_eps = 1e-05
peak_eps = 1e-06


def padded_2(cells, sides, width):
    for axis, dim in sides:
        count = lax.axis_size(axis)
        ends = count - 1
        head = lax.slice_in_dim(cells, 0, width, axis=dim)
        tail = lax.slice_in_dim(cells, cells.shape[dim] - width, cells.shape[dim], axis=dim)
        cells = jnp.concatenate(
            [
                lax.ppermute(tail, axis, [(i, (i + 1) % count) for i in range(ends)]),
                cells,
                lax.ppermute(head, axis, [((i + 1) % count, i) for i in range(ends)]),
            ],
            axis=dim,
        )
    return cells


def smooth_weights(radius):
    weights_raw = [
        math.exp(-(offset * offset) / (2.0 * sigma_smooth * sigma_smooth))
        for offset in range(-radius, radius + 1)
    ]
    weights_total = sum(weights_raw)
    return [weight_one / weights_total for weight_one in weights_raw]


def window_sum(volume, axis_pos, length, weights):
    result = weights[0] * lax.slice_in_dim(volume, 0, length, axis=axis_pos)
    for offset in range(1, len(weights)):
        result = result + weights[offset] * lax.slice_in_dim(
            volume, offset, offset + length, axis=axis_pos
        )
    return result


def boxed_local(extended, block_side, width_y, radius):
    box_ones = [1.0] * (2 * radius + 1)
    padded = jnp.pad(extended, ((0, 0), (0, 0), (radius, radius)))
    result = window_sum(padded, 0, block_side, box_ones)
    result = window_sum(result, 1, block_side, box_ones)
    return window_sum(result, 2, width_y, box_ones)


def per_device(
    fixed_image, moving_image, fetch_owner, fetch_block, fetch_count, interp_level, block_mask
):
    block_side = fixed_image.shape[0]
    width_y = fixed_image.shape[2]
    blocks_dev = fetch_count.shape[2]
    max_list = fetch_owner.shape[3]
    owners = lax.axis_size("blk")
    peer_slots = max(2, (blocks_dev * max_list + owners - 1) // owners)
    entries = blocks_dev * max_list
    voxels = block_side * block_side * block_side
    radius = BOX_RADIUS
    count_box = float((2 * radius + 1) ** 3)
    reach = SMOOTH_RADIUS
    smooth_taps = smooth_weights(reach)
    source_owner = fetch_owner.reshape(entries)
    source_index = fetch_block.reshape(entries)
    list_length = fetch_count.reshape(blocks_dev)
    in_list = (jnp.arange(max_list)[None, :] < list_length[:, None]).reshape(entries)
    owner_hits = ((source_owner[:, None] == jnp.arange(owners)[None, :]) & in_list[:, None]).astype(
        jnp.int32
    )
    hits_before = jnp.cumsum(owner_hits, axis=0) - owner_hits
    owner_rank = jnp.sum(hits_before * owner_hits, axis=1)
    slot_index = jnp.where(in_list, source_owner * peer_slots + owner_rank, -1)
    chooser = slot_index[:, None] == jnp.arange(owners * peer_slots)[None, :]
    wanted = jnp.sum(jnp.where(chooser, source_index[:, None], 0), axis=0).reshape(
        owners, peer_slots
    )
    moving_blocks = (
        moving_image.reshape(block_side, block_side, blocks_dev, block_side)
        .transpose(2, 0, 1, 3)
        .reshape(blocks_dev, voxels)
    )
    selector = (
        lax.all_to_all(wanted, "blk", split_axis=0, concat_axis=0, tiled=True)[:, :, None]
        == jnp.arange(blocks_dev)[None, None, :]
    ).astype(jnp.bfloat16)
    replies = jnp.einsum(
        "ncg,gv->ncv", selector, moving_blocks, preferred_element_type=jnp.float32
    ).astype(jnp.bfloat16)
    fetched = lax.all_to_all(replies, "blk", split_axis=0, concat_axis=0, tiled=True)
    gathered = jnp.dot(
        chooser.astype(jnp.bfloat16),
        fetched.reshape(owners * peer_slots, voxels),
        preferred_element_type=jnp.float32,
    )
    fractions = (
        jnp.swapaxes(interp_level.reshape(blocks_dev, 3, max_list), 1, 2)
        .reshape(entries, 3)
        .astype(jnp.float32)
        / LEVELS
    )
    linear = jnp.arange(voxels)
    position_x = linear // (block_side * block_side)
    position_z = linear // block_side % block_side
    position_y = linear % block_side
    for axis_step, stride, position in (
        (0, block_side * block_side, position_x),
        (1, block_side, position_z),
        (2, 1, position_y),
    ):
        shifted = jnp.concatenate([gathered[:, stride:], gathered[:, :stride]], axis=1)
        shifted = jnp.where((position == block_side - 1)[None, :], gathered, shifted)
        factor = fractions[:, axis_step][:, None]
        gathered = (1.0 - factor) * gathered + factor * shifted
    weights = in_list.astype(jnp.float32) / jnp.repeat(list_length.astype(jnp.float32), max_list)
    warped_blocks = jnp.sum(
        (gathered * weights[:, None]).reshape(blocks_dev, max_list, voxels), axis=1
    )
    warped = (
        warped_blocks.astype(jnp.bfloat16)
        .reshape(blocks_dev, block_side, block_side, block_side)
        .transpose(1, 2, 0, 3)
        .reshape(block_side, block_side, width_y)
    )
    both_ext = padded_2(jnp.stack([fixed_image, warped]), (("slab", 2), ("blk", 1)), radius)
    fixed_f = both_ext[0].astype(jnp.float32)
    fixed_box = boxed_local(fixed_f, block_side, width_y, radius)
    fixed_square = boxed_local(fixed_f * fixed_f, block_side, width_y, radius)
    moving_ext = both_ext[1]
    moving_f = moving_ext.astype(jnp.float32)
    moving_box = boxed_local(moving_f, block_side, width_y, radius)
    moving_square = boxed_local(moving_f * moving_f, block_side, width_y, radius)
    cross_box = boxed_local(fixed_f * moving_f, block_side, width_y, radius)
    mean_fixed = fixed_box / count_box
    mean_moving = moving_box / count_box
    var_fixed = fixed_square / count_box - mean_fixed * mean_fixed + var_eps
    var_moving = moving_square / count_box - mean_moving * mean_moving + var_eps
    covariance = cross_box / count_box - mean_fixed * mean_moving
    center_fixed = fixed_f[radius : radius + block_side, radius : radius + block_side, :]
    center_moving = moving_f[radius : radius + block_side, radius : radius + block_side, :]
    grad_x = (
        moving_f[radius + 1 : radius + 1 + block_side, radius : radius + block_side, :]
        - moving_f[radius - 1 : radius - 1 + block_side, radius : radius + block_side, :]
    ) * 0.5
    grad_z = (
        moving_f[radius : radius + block_side, radius + 1 : radius + 1 + block_side, :]
        - moving_f[radius : radius + block_side, radius - 1 : radius - 1 + block_side, :]
    ) * 0.5
    padded_y = jnp.pad(center_moving, ((0, 0), (0, 0), (1, 1)))
    grad_y = (padded_y[:, :, 2:] - padded_y[:, :, :-2]) * 0.5
    mask_voxel = jnp.repeat(block_mask.reshape(blocks_dev).astype(jnp.float32), block_side)[
        None, None, :
    ]
    scalar_term = (
        mask_voxel
        * 2.0
        * covariance
        / (var_fixed * var_moving)
        * (center_fixed - mean_fixed - covariance / var_moving * (center_moving - mean_moving))
    )
    forces = jnp.stack([scalar_term * grad_x, scalar_term * grad_z, scalar_term * grad_y]).astype(
        jnp.bfloat16
    )
    force_ext = padded_2(forces, (("slab", 2), ("blk", 1)), reach).astype(jnp.float32)
    smooth_now = window_sum(force_ext, 1, block_side, smooth_taps)
    smooth_now = window_sum(smooth_now, 2, block_side, smooth_taps)
    padded_s = jnp.pad(smooth_now, ((0, 0), (0, 0), (0, 0), (reach, reach)))
    smoothed = window_sum(padded_s, 3, width_y, smooth_taps)
    norms = jnp.sqrt(
        smoothed[0] * smoothed[0] + smoothed[1] * smoothed[1] + smoothed[2] * smoothed[2]
    )
    peak_norm = lax.pmax(jnp.max(norms), ("slab", "blk"))
    return step_length * smoothed / (peak_norm + peak_eps)


def solution(mesh):
    in_specs = (
        P("blk", "slab", None),
        P("blk", "slab", None),
        P("blk", "slab", None, None),
        P("blk", "slab", None, None),
        P("blk", "slab", None),
        P("blk", "slab", None, None, None),
        P("blk", "slab", None),
    )
    out_specs = P(None, "blk", "slab", None)
    return jax.shard_map(
        per_device, mesh=mesh, in_specs=in_specs, out_specs=out_specs, check_vma=False
    )
```

profile of v0, /device:TPU:0, one launch (start us, length us, event | category | flops | bytes accessed | tf_op | source)
XLA Modules:
  0.0 147.0 jit_solution(15901855817269786074)
XLA Ops:
  0.0 0.8 reshape.153
  0.8 0.8 broadcast_in_dim.54
  1.5 0.7 iota_compare_fusion.5
  2.7 0.7 all_to_all.9
  3.4 5.2 %all-to-all-start = ((s32[8,1,2]{2,1,0:T(1,128)}), s32[8,1,2]{2,1,0:T(1,128)S(1)}, u32[]{:S(2)}, u32[]{:S(2)}) async-start(s32[8,1,2]{2,1,0:T(1,128)} %bitcast.8), calls=%async_computation | async-start | bytes 8192 | tf_op jit(solution)/shard_map/all_to_all | solution.py:97
  8.6 0.7 bitcast_convert_fusion
  9.4 0.7 multiply_bitcast_fusion
  10.2 2.1 %reshape.154 = bf16[32,32,4,32]{3,2,1,0:T(4,128)(2,1)S(1)} reshape(bf16[32,32,128]{2,1,0:T(8,128)(2,1)} %param.8) | data formatting | bytes 524288 | tf_op jit(solution)/shard_map/reshape | solution.py:92
  12.5 1.1 reshape.161
  13.6 0.5 convolution_convert_fusion
  14.1 2.0 %copy.25 = bf16[8,2,32768]{2,1,0:T(2,128)(2,1)} copy(bf16[8,2,32768]{2,0,1:T(8,128)(2,1)S(1)} %convolution_convert_fusion) | data formatting | bytes 2097152 | tf_op jit(solution)/shard_map/convert_element_type | solution.py:102
  16.2 4.2 %all-to-all-start.1 = ((bf16[8,2,32768]{2,1,0:T(2,128)(2,1)}), bf16[8,2,32768]{2,1,0:T(2,128)(2,1)S(1)}, u32[]{:S(2)}, u32[]{:S(2)}) async-start(bf16[8,2,32768]{2,1,0:T(2,128)(2,1)} %copy.25), calls=%async_computation.1 | async-start | bytes 2097152 | tf_op jit(solution)/shard_map/all_to_all | solution.py:103
  20.4 15.3 %all-to-all-done.1 = bf16[8,2,32768]{2,1,0:T(2,128)(2,1)S(1)} async-done(((bf16[8,2,32768]{2,1,0:T(2,128)(2,1)}), bf16[8,2,32768]{2,1,0:T(2,128)(2,1)S(1)}, u32[]{:S(2)}, u32[]{:S(2)}) %all-to-all-start.1) | async-done | bytes 1048608 | tf_op jit(solution)/shard_map/all_to_all | solution.py:103
  35.8 0.4 reshape.156
  36.2 0.5 fusion.98
  37.3 0.6 slice.506
  37.9 0.5 fusion.3
  38.4 0.6 slice.508
  39.0 1.8 %fusion.6 = f32[16,32768]{1,0:T(8,128)} fusion(f32[16,32768]{1,0:T(8,128)S(1)} %fusion.3, f32[16,1]{1,0:T(8,128)S(1)} %slice.509, f32[16,32767]{1,0:T(8,128)S(1)} %slice.508, f32[16]{0:T(128)S(1)} %convert_divide_fusion, f32[16]{0:T(128)S(1)} %get-tuple-element.23, f32[16]{0:T(128)S(1)} %get-tuple-element.22, pred[32768]{0:T(1024)(128)(4,1)S(1)} %fusion.94), kind=kLoop, calls=%fused_computation.41 | loop fusion | flops 3145728 | bytes 6324416 | tf_op jit(solution)/shard_map/mul | solution.py:130
  40.8 1.9 %reshape.158 = f32[4,4,32768]{2,1,0:T(4,128)S(1)} reshape(f32[16,32768]{1,0:T(8,128)} %fusion.6) | data formatting | bytes 4194304 | tf_op jit(solution)/shard_map/reshape | solution.py:130
  42.7 1.5 %reduce_sum.29 = bf16[4,32768]{1,0:T(4,128)(2,1)S(1)} reduce(f32[4,4,32768]{2,1,0:T(4,128)S(1)} %reshape.158, f32[]{:T(128)} %constant.86.clone.1), dimensions={1}, to_apply=%region_3.4 | reduce | flops 393216 | bytes 2359300 | tf_op jit(solution)/shard_map/reduce_sum | solution.py:129
  44.2 0.6 convert_element_type.68
  44.8 0.8 copy.26
  45.6 0.5 stack_reshape.3
  46.2 3.5 %collective-permute-start = (bf16[2,32,2,128]{3,2,1,0:T(2,128)(2,1)S(1)}, bf16[2,32,2,128]{3,2,1,0:T(2,128)(2,1)S(1)}, u32[]{:S(2)}, u32[]{:S(2)}) collective-permute-start(bf16[2,32,2,128]{3,2,1,0:T(2,128)(2,1)S(1)} %get-tuple-element.20), channel_id=1, source_target_pairs={{0,8},{8,16},{16,24},{1,9},{9,17},{17,25},{2,10},{10,18},{18,26},{... | collective-permute-start | bytes 98312 | tf_op jit(solution)/shard_map/ppermute | solution.py:27
  49.7 1.3 collective-permute-start.1
  51.3 4.2 %collective-permute-done.1 = bf16[2,32,2,128]{3,2,1,0:T(2,128)(2,1)S(1)} collective-permute-done((bf16[2,32,2,128]{3,2,1,0:T(2,128)(2,1)S(1)}, bf16[2,32,2,128]{3,2,1,0:T(2,128)(2,1)S(1)}, u32[]{:S(2)}, u32[]{:S(2)}) %collective-permute-start.1) | collective-permute-done | bytes 32800 | tf_op jit(solution)/shard_map/ppermute | solution.py:29
  55.6 1.3 collective-permute-start.2
  56.9 1.5 %collective-permute-start.3 = (bf16[2,2,36,128]{3,2,1,0:T(8,128)(2,1)S(1)}, bf16[2,2,36,128]{3,2,1,0:T(8,128)(2,1)S(1)}, u32[]{:S(2)}, u32[]{:S(2)}) collective-permute-start(bf16[2,2,36,128]{3,2,1,0:T(8,128)(2,1)S(1)} %get-tuple-element.19), channel_id=1, source_target_pairs={{1,0},{2,1},{3,2},{4,3},{5,4},{6,5},{7,6},{9,8},{10,9},{11,10},{12... | collective-permute-start | bytes 110600 | tf_op jit(solution)/shard_map/ppermute | solution.py:29
  58.5 2.2 %collective-permute-done.3 = bf16[2,2,36,128]{3,2,1,0:T(8,128)(2,1)S(1)} collective-permute-done((bf16[2,2,36,128]{3,2,1,0:T(8,128)(2,1)S(1)}, bf16[2,2,36,128]{3,2,1,0:T(8,128)(2,1)S(1)}, u32[]{:S(2)}, u32[]{:S(2)}) %collective-permute-start.3) | collective-permute-done | bytes 36896 | tf_op jit(solution)/shard_map/ppermute | solution.py:29
  61.3 3.4 %fusion.34 = (f32[32,36,132]{2,1,0:T(8,128)S(1)}, f32[32,36,132]{2,1,0:T(8,128)S(1)}) fusion(f32[36,36,128]{2,1,0:T(8,128)S(1)} %get-tuple-element.13, f32[36,36,128]{2,1,0:T(8,128)S(1)} %get-tuple-element.15), kind=kLoop, calls=%fused_computation.84 | loop fusion | flops 1216512 | bytes 2543616 | tf_op jit(solution)/shard_map/add | solution.py:48
  65.6 1.7 %fusion.50 = f32[32,36,132]{2,1,0:T(8,128)S(1)} fusion(f32[36,36,128]{2,1,0:T(8,128)S(1)} %get-tuple-element.14), kind=kLoop, calls=%fused_computation.100 | loop fusion | flops 608256 | bytes 1271808 | tf_op jit(solution)/shard_map/add | solution.py:48
  67.8 3.4 %fusion.38 = (f32[32,36,132]{2,1,0:T(8,128)S(1)}, f32[32,36,132]{2,1,0:T(8,128)S(1)}) fusion(f32[36,36,128]{2,1,0:T(8,128)S(1)} %get-tuple-element.16, f32[36,36,128]{2,1,0:T(8,128)S(1)} %get-tuple-element.17), kind=kLoop, calls=%fused_computation.88 | loop fusion | flops 1216512 | bytes 2543616 | tf_op jit(solution)/shard_map/add | solution.py:48
  72.0 3.0 %fusion.84 = (bf16[1,32,32,128]{3,2,1,0:T(8,128)(2,1)S(1)}, f32[32,32,128]{2,1,0:T(8,128)S(1)}) fusion(f32[36,36,128]{2,1,0:T(8,128)S(1)} %get-tuple-element.17, f32[36,36,128]{2,1,0:T(8,128)S(1)} %get-tuple-element.16, f32[32,32,132]{2,1,0:T(8,128)S(1)} %slice_add_fusion, f32[32,32,132]{2,1,0:T(8,128)S(1)} %slice_add_fusion.4, ...), kind=kLoop, calls=%fused_computation.186 | loop fusion | flops 6029312 | bytes 15991296 | tf_op jit(solution)/shard_map/stack | solution.py:174
  75.6 3.5 %collective-permute-start.4 = (bf16[3,32,3,128]{3,2,1,0:T(4,128)(2,1)S(1)}, bf16[3,32,3,128]{3,2,1,0:T(4,128)(2,1)S(1)}, u32[]{:S(2)}, u32[]{:S(2)}) collective-permute-start(bf16[3,32,3,128]{3,2,1,0:T(4,128)(2,1)S(1)} %get-tuple-element.9), channel_id=1, source_target_pairs={{0,8},{8,16},{16,24},{1,9},{9,17},{17,25},{2,10},{10,18},{18,26},{... | collective-permute-start | bytes 221192 | tf_op jit(solution)/shard_map/ppermute | solution.py:27
  79.1 1.3 collective-permute-start.5
  80.4 0.9 collective-permute-done.4
  81.3 4.3 %collective-permute-done.5 = bf16[3,32,3,128]{3,2,1,0:T(4,128)(2,1)S(1)} collective-permute-done((bf16[3,32,3,128]{3,2,1,0:T(4,128)(2,1)S(1)}, bf16[3,32,3,128]{3,2,1,0:T(4,128)(2,1)S(1)}, u32[]{:S(2)}, u32[]{:S(2)}) %collective-permute-start.5) | collective-permute-done | bytes 73760 | tf_op jit(solution)/shard_map/ppermute | solution.py:29
  85.7 3.2 %collective-permute-start.6 = (bf16[3,3,38,128]{3,2,1,0:T(8,128)(2,1)S(1)}, bf16[3,3,38,128]{3,2,1,0:T(8,128)(2,1)S(1)}, u32[]{:S(2)}, u32[]{:S(2)}) collective-permute-start(bf16[3,3,38,128]{3,2,1,0:T(8,128)(2,1)S(1)} %get-tuple-element.7), channel_id=1, source_target_pairs={{0,1},{1,2},{2,3},{3,4},{4,5},{5,6},{6,7},{8,9},{9,10},{10,11},{11... | collective-permute-start | bytes 262664 | tf_op jit(solution)/shard_map/ppermute | solution.py:27
  88.9 1.5 %collective-permute-start.7 = (bf16[3,3,38,128]{3,2,1,0:T(8,128)(2,1)S(1)}, bf16[3,3,38,128]{3,2,1,0:T(8,128)(2,1)S(1)}, u32[]{:S(2)}, u32[]{:S(2)}) collective-permute-start(bf16[3,3,38,128]{3,2,1,0:T(8,128)(2,1)S(1)} %get-tuple-element.8), channel_id=1, source_target_pairs={{1,0},{2,1},{3,2},{4,3},{5,4},{6,5},{7,6},{9,8},{10,9},{11,10},{12... | collective-permute-start | bytes 262664 | tf_op jit(solution)/shard_map/ppermute | solution.py:29
  90.4 2.6 %collective-permute-done.7 = bf16[3,3,38,128]{3,2,1,0:T(8,128)(2,1)S(1)} collective-permute-done((bf16[3,3,38,128]{3,2,1,0:T(8,128)(2,1)S(1)}, bf16[3,3,38,128]{3,2,1,0:T(8,128)(2,1)S(1)}, u32[]{:S(2)}, u32[]{:S(2)}) %collective-permute-start.7) | collective-permute-done | bytes 87584 | tf_op jit(solution)/shard_map/ppermute | solution.py:29
  93.0 0.4 maximum_convert_fusion
  93.4 0.7 fusion.7
  94.1 1.3 fusion.25
  95.4 2.5 %fusion.19 = f32[3,32,32,128]{3,2,1,0:T(8,128)S(1)} fusion(f32[3,32,32,128]{3,2,1,0:T(8,128)S(1)} %fusion.25), kind=kLoop, calls=%fused_computation.61 | loop fusion | flops 5111808 | bytes 3145728 | tf_op jit(solution)/shard_map/add | solution.py:48
  97.9 0.8 fusion.57
  98.7 44.0 %pmax.7 = f32[]{:T(128)} all-reduce(f32[]{:T(128)} %fusion.57), channel_id=1, replica_groups=mesh['slab'=4,'blk'=8] {'slab','blk'}, use_global_device_ids=true, to_apply=%region_5.6 | all-reduce | flops 1 | bytes 8 | tf_op jit(solution)/shard_map/pmax | solution.py:185
  143.3 3.6 %multiply_divide_fusion = f32[3,32,32,128]{3,2,1,0:T(8,128)} fusion(f32[]{:T(128)S(6)} %add.397, f32[3,32,32,128]{3,2,1,0:T(8,128)S(1)} %fusion.25), kind=kLoop, calls=%fused_computation.80 | loop fusion | flops 5898240 | bytes 3145732 | tf_op jit(solution)/shard_map/div | solution.py:186
  (46 shorter events, 5.5 us)
Async XLA Ops:
  3.4 10.1 %all-to-all-start = ((s32[8,1,2]{2,1,0:T(1,128)}), s32[8,1,2]{2,1,0:T(1,128)S(1)}, u32[]{:S(2)}, u32[]{:S(2)}) async-start(s32[8,1,2]{2,1,0:T(1,128)} %bitcast.8), calls=%async_computation | async-start | bytes 8192 | tf_op jit(solution)/shard_map/all_to_all | solution.py:97
  16.2 19.6 %all-to-all-start.1 = ((bf16[8,2,32768]{2,1,0:T(2,128)(2,1)}), bf16[8,2,32768]{2,1,0:T(2,128)(2,1)S(1)}, u32[]{:S(2)}, u32[]{:S(2)}) async-start(bf16[8,2,32768]{2,1,0:T(2,128)(2,1)} %copy.25), calls=%async_computation.1 | async-start | bytes 2097152 | tf_op jit(solution)/shard_map/all_to_all | solution.py:103
  44.8 1.4 copy-start
  45.6 12.7 %copy-start.1 = (s32[1,1,4]{2,1,0:T(1,128)S(1)}, s32[1,1,4]{2,1,0:T(1,128)}, u32[]{:S(2)}) copy-start(s32[1,1,4]{2,1,0:T(1,128)} %param.13) | copy-start | bytes 52
  46.2 5.1 %collective-permute-start = (bf16[2,32,2,128]{3,2,1,0:T(2,128)(2,1)S(1)}, bf16[2,32,2,128]{3,2,1,0:T(2,128)(2,1)S(1)}, u32[]{:S(2)}, u32[]{:S(2)}) collective-permute-start(bf16[2,32,2,128]{3,2,1,0:T(2,128)(2,1)S(1)} %get-tuple-element.20), channel_id=1, source_target_pairs={{0,8},{8,16},{16,24},{1,9},{9,17},{17,25},{2,10},{10,18},{18,26},{... | collective-permute-start | bytes 98312 | tf_op jit(solution)/shard_map/ppermute | solution.py:27
  49.7 5.8 %collective-permute-start.1 = (bf16[2,32,2,128]{3,2,1,0:T(2,128)(2,1)S(1)}, bf16[2,32,2,128]{3,2,1,0:T(2,128)(2,1)S(1)}, u32[]{:S(2)}, u32[]{:S(2)}) collective-permute-start(bf16[2,32,2,128]{3,2,1,0:T(2,128)(2,1)S(1)} %get-tuple-element.21), channel_id=1, source_target_pairs={{8,0},{16,8},{24,16},{9,1},{17,9},{25,17},{10,2},{18,10},{26,18},{... | collective-permute-start | bytes 98312 | tf_op jit(solution)/shard_map/ppermute | solution.py:29
  55.6 3.0 %collective-permute-start.2 = (bf16[2,2,36,128]{3,2,1,0:T(8,128)(2,1)S(1)}, bf16[2,2,36,128]{3,2,1,0:T(8,128)(2,1)S(1)}, u32[]{:S(2)}, u32[]{:S(2)}) collective-permute-start(bf16[2,2,36,128]{3,2,1,0:T(8,128)(2,1)S(1)} %get-tuple-element.18), channel_id=1, source_target_pairs={{0,1},{1,2},{2,3},{3,4},{4,5},{5,6},{6,7},{8,9},{9,10},{10,11},{11... | collective-permute-start | bytes 110600 | tf_op jit(solution)/shard_map/ppermute | solution.py:27
  56.9 3.9 %collective-permute-start.3 = (bf16[2,2,36,128]{3,2,1,0:T(8,128)(2,1)S(1)}, bf16[2,2,36,128]{3,2,1,0:T(8,128)(2,1)S(1)}, u32[]{:S(2)}, u32[]{:S(2)}) collective-permute-start(bf16[2,2,36,128]{3,2,1,0:T(8,128)(2,1)S(1)} %get-tuple-element.19), channel_id=1, source_target_pairs={{1,0},{2,1},{3,2},{4,3},{5,4},{6,5},{7,6},{9,8},{10,9},{11,10},{12... | collective-permute-start | bytes 110600 | tf_op jit(solution)/shard_map/ppermute | solution.py:29
  75.6 5.7 %collective-permute-start.4 = (bf16[3,32,3,128]{3,2,1,0:T(4,128)(2,1)S(1)}, bf16[3,32,3,128]{3,2,1,0:T(4,128)(2,1)S(1)}, u32[]{:S(2)}, u32[]{:S(2)}) collective-permute-start(bf16[3,32,3,128]{3,2,1,0:T(4,128)(2,1)S(1)} %get-tuple-element.9), channel_id=1, source_target_pairs={{0,8},{8,16},{16,24},{1,9},{9,17},{17,25},{2,10},{10,18},{18,26},{... | collective-permute-start | bytes 221192 | tf_op jit(solution)/shard_map/ppermute | solution.py:27
  79.1 6.5 %collective-permute-start.5 = (bf16[3,32,3,128]{3,2,1,0:T(4,128)(2,1)S(1)}, bf16[3,32,3,128]{3,2,1,0:T(4,128)(2,1)S(1)}, u32[]{:S(2)}, u32[]{:S(2)}) collective-permute-start(bf16[3,32,3,128]{3,2,1,0:T(4,128)(2,1)S(1)} %get-tuple-element.10), channel_id=1, source_target_pairs={{8,0},{16,8},{24,16},{9,1},{17,9},{25,17},{10,2},{18,10},{26,18},{... | collective-permute-start | bytes 221192 | tf_op jit(solution)/shard_map/ppermute | solution.py:29
  85.7 4.7 %collective-permute-start.6 = (bf16[3,3,38,128]{3,2,1,0:T(8,128)(2,1)S(1)}, bf16[3,3,38,128]{3,2,1,0:T(8,128)(2,1)S(1)}, u32[]{:S(2)}, u32[]{:S(2)}) collective-permute-start(bf16[3,3,38,128]{3,2,1,0:T(8,128)(2,1)S(1)} %get-tuple-element.7), channel_id=1, source_target_pairs={{0,1},{1,2},{2,3},{3,4},{4,5},{5,6},{6,7},{8,9},{9,10},{10,11},{11... | collective-permute-start | bytes 262664 | tf_op jit(solution)/shard_map/ppermute | solution.py:27
  88.9 4.1 %collective-permute-start.7 = (bf16[3,3,38,128]{3,2,1,0:T(8,128)(2,1)S(1)}, bf16[3,3,38,128]{3,2,1,0:T(8,128)(2,1)S(1)}, u32[]{:S(2)}, u32[]{:S(2)}) collective-permute-start(bf16[3,3,38,128]{3,2,1,0:T(8,128)(2,1)S(1)} %get-tuple-element.8), channel_id=1, source_target_pairs={{1,0},{2,1},{3,2},{4,3},{5,4},{6,5},{7,6},{9,8},{10,9},{11,10},{12... | collective-permute-start | bytes 262664 | tf_op jit(solution)/shard_map/ppermute | solution.py:29
where the time goes:
time: 148 us; the launch traced here: 147 us
  blocking collectives  44 us (30%)
  other arithmetic  31.1 us (21%)
  waiting for transfers between devices  29.8 us (20%)
  starting transfers between devices  26.4 us (18%)
  local copies, waits for them, and re-layouts  13.6 us (9%)
    pmax x1, blocking collectives, per_device(): peak_norm = lax.pmax(jnp.max(norms), ('slab', 'blk'))  44 us
    all_to_all x1, waiting for transfers between devices, per_device(): lax.all_to_all(replies, 'blk', split_axis=0, concat_axis=0, tiled=True)  15.3 us
    add x11, other arithmetic, window_sum(): result + weights[offset] * lax.slice_in_dim(volume, offset, offset + leng...  15.1 us
    ppermute x4, waiting for transfers between devices, padded_2(): lax.ppermute(head, axis, [((i + 1) % count, i) for i in range(ends)])  13.3 us
    ppermute x4, starting transfers between devices, padded_2(): lax.ppermute(tail, axis, [(i, (i + 1) % count) for i in range(ends)])  11.4 us
    ppermute x4, starting transfers between devices, padded_2(): lax.ppermute(head, axis, [((i + 1) % count, i) for i in range(ends)])  5.57 us
    all_to_all x1, starting transfers between devices, per_device(): lax.all_to_all(wanted, 'blk', split_axis=0, concat_axis=0, tiled=True)  5.17 us
    all_to_all x1, starting transfers between devices, per_device(): lax.all_to_all(replies, 'blk', split_axis=0, concat_axis=0, tiled=True)  4.2 us
  transfers between devices with their start and end apart: 10, of which 7 were waited for; matrix products, arithmetic and copies ran while one was open for 3% of the time, Pallas kernels for 0%

commit v1 on v0

v1 whole, which is shorter than its diff:
```python
import functools
import math

import jax
import jax.numpy as jnp
from jax import lax
from jax.experimental import pallas as pl
from jax.experimental.pallas import tpu as pltpu
from jax.sharding import PartitionSpec as P

LEVELS = 8
BOX_RADIUS = 2
SMOOTH_RADIUS = 3
HALO = BOX_RADIUS + SMOOTH_RADIUS

sigma_smooth = 1.5
step_length = 2.0
var_eps = 1e-05
peak_eps = 1e-06

SIDE = 32
LANES = 128
PLANES = SIDE + 2 * HALO
ROWS = 48
FIRST = 8
FPLANES = SIDE + 2 * SMOOTH_RADIUS
FROWS = 40
F32 = jnp.float32
BF16 = jnp.bfloat16
MESH = pl.DeviceIdType.MESH
DIRECTIONS = ((1, 0), (-1, 0), (0, 1), (0, -1), (1, 1), (1, -1), (-1, 1), (-1, -1))


def smooth_weights(radius):
    weights_raw = [
        math.exp(-(offset * offset) / (2.0 * sigma_smooth * sigma_smooth))
        for offset in range(-radius, radius + 1)
    ]
    weights_total = sum(weights_raw)
    return [weight_one / weights_total for weight_one in weights_raw]


def kernel(
    n_slab,
    n_blk,
    fixed_ref,
    moving_ref,
    owner_ref,
    block_ref,
    count_ref,
    level_ref,
    mask_ref,
    out_ref,
    scale_ref,
    gath,
    select,
    acc,
    f_ext,
    m_ext,
    ybuf,
    zbox,
    f_mean,
    f_inv,
    f_dev,
    grad_y,
    forces,
    ysm,
    zsm,
    mask_pl,
    band_m,
    band_2,
    band_s,
    fx_send,
    fz_send,
    fx_recv,
    fz_recv,
    fc_recv,
    mx_send,
    mz_send,
    mx_recv,
    mz_recv,
    mc_recv,
    pk_send,
    pk_blk,
    pk_slab,
    ag_ssem,
    ag_rsem,
    f_ssem,
    f_rsem,
    m_ssem,
    m_rsem,
    pb_ssem,
    pb_rsem,
    ps_ssem,
    ps_rsem,
):
    me_s = lax.axis_index("slab")
    me_b = lax.axis_index("blk")
    chips = n_blk // 2
    chip = me_b // 2
    core = me_b % 2
    taps = smooth_weights(SMOOTH_RADIUS)

    def there(dx, dz):
        ok = None
        for d, me, n in ((dx, me_b, n_blk), (dz, me_s, n_slab)):
            if d == 0:
                continue
            now = me + d < n if d > 0 else me + d >= 0
            ok = now if ok is None else jnp.logical_and(ok, now)
        return ok

    barrier = pltpu.get_barrier_semaphore()
    for d in range(1, n_blk):
        pl.semaphore_signal(
            barrier, inc=1, device_id=(me_s, (me_b + d) % n_blk), device_id_type=MESH
        )
    for d in range(1, n_slab):
        pl.semaphore_signal(
            barrier, inc=1, device_id=((me_s + d) % n_slab, me_b), device_id_type=MESH
        )
    for dx, dz in DIRECTIONS[4:]:

        @pl.when(there(dx, dz))
        def _():
            pl.semaphore_signal(
                barrier, inc=1, device_id=(me_s + dz, me_b + dx), device_id_type=MESH
            )

    wide_x = jnp.where(me_b > 0, 1, 0) + jnp.where(me_b < n_blk - 1, 1, 0)
    wide_z = jnp.where(me_s > 0, 1, 0) + jnp.where(me_s < n_slab - 1, 1, 0)
    pl.semaphore_wait(barrier, n_blk - 1 + n_slab - 1 + wide_x * wide_z)

    def spread(e):
        return pltpu.make_async_remote_copy(
            src_ref=moving_ref,
            dst_ref=gath.at[2 * e],
            send_sem=ag_ssem.at[2 * e],
            recv_sem=ag_rsem.at[2 * e],
            device_id=(me_s, 2 * ((chip + e) % chips) + core),
            device_id_type=MESH,
        )

    def to_sibling(e):
        return pltpu.make_async_remote_copy(
            src_ref=moving_ref if e == 0 else gath.at[2 * e],
            dst_ref=gath.at[2 * e + 1],
            send_sem=ag_ssem.at[2 * e + 1],
            recv_sem=ag_rsem.at[2 * e + 1],
            device_id=(me_s, 2 * chip + 1 - core),
            device_id_type=MESH,
        )

    for e in range(1, chips):
        spread(e).start()
    to_sibling(0).start()

    def rim_copies(x_send, z_send, x_recv, z_recv, c_recv, ssem, rsem):
        copies = []
        for i, (dx, dz) in enumerate(DIRECTIONS):
            if dz == 0:
                src, dst = x_send.at[(dx + 1) // 2], x_recv.at[(dx + 1) // 2]
            elif dx == 0:
                src, dst = z_send.at[(dz + 1) // 2], z_recv.at[(dz + 1) // 2]
            else:
                src = z_send.at[(dz + 1) // 2, :, pl.ds(16 if dx > 0 else 0, 16), :]
                dst = c_recv.at[i - 4]
            copies.append(
                pltpu.make_async_remote_copy(
                    src_ref=src,
                    dst_ref=dst,
                    send_sem=ssem.at[i],
                    recv_sem=rsem.at[i],
                    device_id=(me_s + dz, me_b + dx),
                    device_id_type=MESH,
                )
            )
        return copies

    def start_all(copies):
        for (dx, dz), copy in zip(DIRECTIONS, copies):
            pl.when(there(dx, dz))(copy.start)

    def finish_all(copies):
        for (dx, dz), copy in zip(DIRECTIONS, copies):
            pl.when(there(dx, dz))(copy.wait_send)

    def pack_rims(ext, x_send, z_send):
        flat = ext.reshape(PLANES * ROWS, LANES)
        for j in range(HALO):
            for side, at in ((0, j), (1, SIDE - HALO + j)):
                z_send[side, j] = flat[
                    pl.ds(HALO * ROWS + FIRST + at, SIDE, stride=ROWS), :
                ].astype(BF16)
                x_send[side, j] = ext[HALO + at, FIRST : FIRST + SIDE, :].astype(BF16)

    def fill_rims(copies, ext, x_recv, z_recv, c_recv, mask):
        flat = ext.reshape(PLANES * ROWS, LANES)
        for i, (dx, dz) in enumerate(DIRECTIONS):
            at_x = 0 if dx > 0 else HALO + SIDE
            at_z = FIRST - HALO if dz > 0 else FIRST + SIDE
            region = {1: 0, 0: 1, -1: 2}[dx]
            row_at = {1: 0, 0: SMOOTH_RADIUS, -1: SMOOTH_RADIUS + SIDE}[dz]
            row_n = SIDE if dz == 0 else SMOOTH_RADIUS

            @pl.when(there(-dx, -dz))
            def _():
                copies[i].wait_recv()
                side_x, side_z = (dx + 1) // 2, (dz + 1) // 2
                for j in range(HALO):
                    if dz == 0:
                        ext[at_x + j, FIRST : FIRST + SIDE, :] = x_recv[side_x, j].astype(F32)
                    elif dx == 0:
                        flat[pl.ds(HALO * ROWS + at_z + j, SIDE, stride=ROWS), :] = z_recv[
                            side_z, j
                        ].astype(F32)
                    else:
                        rows = c_recv[i - 4, j].astype(F32)
                        rows = rows[16 - HALO :] if dx > 0 else rows[:HALO]
                        flat[pl.ds(at_x * ROWS + at_z + j, HALO, stride=ROWS), :] = rows
                if mask:
                    if dz == 0:
                        plane = x_recv[side_x, HALO].astype(F32)
                    elif dx == 0:
                        plane = z_recv[side_z, HALO].astype(F32)
                    else:
                        plane = c_recv[i - 4, HALO].astype(F32)
                    mask_pl[region, row_at : row_at + row_n, :] = plane[:row_n]

    lane = lax.broadcasted_iota(jnp.int32, (1, LANES), 1)

    def by_block(scalars):
        vec = jnp.full((1, LANES), scalars[3], jnp.int32)
        for g in range(3):
            vec = jnp.where(lane // SIDE == g, scalars[g], vec)
        return vec

    for ext in (f_ext, m_ext):

        @pl.loop(0, PLANES)
        def _(x):
            ext[x] = jnp.zeros((ROWS, LANES), F32)

    mask_pl[...] = jnp.zeros_like(mask_pl)
    own_mask = by_block([mask_ref[0, 0, g] for g in range(4)]).astype(F32)
    mask_rows = jnp.broadcast_to(own_mask, (SIDE, LANES))
    mask_pl[1, SMOOTH_RADIUS : SMOOTH_RADIUS + SIDE, :] = mask_rows

    @pl.loop(0, SIDE)
    def _(x):
        f_ext[HALO + x, FIRST : FIRST + SIDE, :] = fixed_ref[x].astype(F32)

    pack_rims(f_ext, fx_send, fz_send)
    for side in range(2):
        fx_send[side, HALO] = mask_rows.astype(BF16)
        fz_send[side, HALO] = mask_rows.astype(BF16)
    f_copies = rim_copies(fx_send, fz_send, fx_recv, fz_recv, fc_recv, f_ssem, f_rsem)
    start_all(f_copies)

    place, frac_x, frac_y, frac_z, weight = [], [], [], [], []
    counts = by_block([count_ref[0, 0, g] for g in range(4)])
    for k in range(4):
        fracs = [
            by_block([level_ref[0, 0, g, a, k] for g in range(4)]).astype(F32) / LEVELS
            for a in range(3)
        ]
        frac_x.append(fracs[0])
        frac_z.append(fracs[1])
        frac_y.append(fracs[2])
        place.append(
            by_block([owner_ref[0, 0, g, k] for g in range(4)]) * LANES
            + by_block([block_ref[0, 0, g, k] for g in range(4)]) * SIDE
            + lane % SIDE
        )
        weight.append(jnp.where(counts > k, 1.0, 0.0) / counts.astype(F32))
    sub = lax.broadcasted_iota(jnp.int32, (LANES, LANES), 0)
    for e in range(chips):
        for p in range(2):
            base = (2 * ((chip + chips - e) % chips) + (core if p == 0 else 1 - core)) * LANES
            for k in range(4):
                first = place[k] - base
                second = first + jnp.where(lane % SIDE == SIDE - 1, 0, 1)
                f_y = frac_y[k]
                select[e, p * LANES : (p + 1) * LANES, k * LANES : (k + 1) * LANES] = (
                    jnp.where(sub == first, 1.0 - f_y, 0.0) + jnp.where(sub == second, f_y, 0.0)
                ).astype(BF16)

    off = sub - lax.broadcasted_iota(jnp.int32, (LANES, LANES), 1)
    band = jnp.where(jnp.abs(off) <= BOX_RADIUS, 1.0, 0.0).astype(BF16)
    band_m[:, :LANES] = band
    band_m[:, LANES:] = (
        jnp.where(off == 1, 0.5, 0.0) - jnp.where(off == -1, 0.5, 0.0)
    ).astype(BF16)
    band_2[:LANES] = band
    band_2[LANES:] = band
    bell = jnp.zeros((LANES, LANES), F32)
    for t in range(2 * SMOOTH_RADIUS + 1):
        bell = jnp.where(off == t - SMOOTH_RADIUS, taps[t], bell)
    bell_hi = bell.astype(BF16)
    band_s[:, :LANES] = bell_hi
    band_s[:, LANES:] = (bell - bell_hi.astype(F32)).astype(BF16)

    def halves(product):
        high = product.astype(BF16)
        return jnp.concatenate([high, (product - high.astype(F32)).astype(BF16)], axis=1)

    def z_sum(ref, q, j):
        total = ref[q, j, 3 : 3 + FROWS, :]
        for t in range(1, 5):
            total = total + ref[q, j, 3 + t : 3 + t + FROWS, :]
        return total

    def x_sum(q, i):
        total = zbox[q, i]
        for t in range(1, 5):
            total = total + zbox[q, i + t]
        return total

    count_box = float((2 * BOX_RADIUS + 1) ** 3)
    group = 7

    fill_rims(f_copies, f_ext, fx_recv, fz_recv, fc_recv, True)

    @pl.loop(0, PLANES // group)
    def _(step):
        planes = f_ext[pl.ds(step * group, group)].reshape(group * ROWS, LANES)
        y_f = jnp.dot(planes.astype(BF16), band, preferred_element_type=F32)
        y_ff = jnp.dot(halves(planes * planes), band_2[...], preferred_element_type=F32)
        ybuf[0] = y_f.reshape(group, ROWS, LANES)
        ybuf[1] = y_ff.reshape(group, ROWS, LANES)
        for j in range(group):
            for q in range(2):
                zbox[q, step * group + j] = z_sum(ybuf, q, j)

    @pl.loop(0, FPLANES)
    def _(i):
        mean = x_sum(0, i) / count_box
        var = x_sum(1, i) / count_box - mean * mean + var_eps
        f_mean[i] = mean
        f_inv[i] = 1.0 / var
        f_dev[i] = f_ext[i + 2, 5 : 5 + FROWS, :] - mean

    @pl.loop(0, SIDE)
    def _(x):
        gath[0, x] = moving_ref[x]

    for e in range(chips):
        if e > 0:
            spread(e).wait_recv()
            to_sibling(e).start()
    for e in range(chips):
        to_sibling(e).wait_recv()

        @pl.loop(0, 4)
        def _(part):
            at = pl.ds(part * 8, 8)
            pair = jnp.concatenate(
                [gath[2 * e, at].reshape(256, LANES), gath[2 * e + 1, at].reshape(256, LANES)],
                axis=1,
            )
            got = jnp.dot(pair, select[e], preferred_element_type=F32)
            rows = pl.ds(part * 256, 256)
            if e == 0:
                acc[rows, :] = got
            else:
                acc[rows, :] = acc[rows, :] + got

    last_row = lax.broadcasted_iota(jnp.int32, (SIDE, LANES), 0) == SIDE - 1

    @pl.loop(0, SIDE)
    def _(x):
        here = pl.ds(pl.multiple_of(x * SIDE, SIDE), SIDE)
        after = pl.ds(pl.multiple_of(jnp.minimum(x + 1, SIDE - 1) * SIDE, SIDE), SIDE)
        stay = jnp.zeros((SIDE, LANES), F32)
        move = jnp.zeros((SIDE, LANES), F32)
        for k in range(4):
            cols = slice(k * LANES, (k + 1) * LANES)
            mixed = (1.0 - frac_x[k]) * acc[here, cols] + frac_x[k] * acc[after, cols]
            stay = stay + (weight[k] * (1.0 - frac_z[k])) * mixed
            move = move + (weight[k] * frac_z[k]) * mixed
        moved = jnp.where(last_row, move, pltpu.roll(move, SIDE - 1, 0))
        m_ext[HALO + x, FIRST : FIRST + SIDE, :] = (stay + moved).astype(BF16).astype(F32)

    pack_rims(m_ext, mx_send, mz_send)
    m_copies = rim_copies(mx_send, mz_send, mx_recv, mz_recv, mc_recv, m_ssem, m_rsem)
    start_all(m_copies)
    fill_rims(m_copies, m_ext, mx_recv, mz_recv, mc_recv, False)

    @pl.loop(0, PLANES // group)
    def _(step):
        at = pl.ds(step * group, group)
        m_now = m_ext[at].reshape(group * ROWS, LANES)
        f_now = f_ext[at].reshape(group * ROWS, LANES)
        y_m = jnp.dot(m_now.astype(BF16), band_m[...], preferred_element_type=F32)
        products = jnp.concatenate([halves(m_now * m_now), halves(f_now * m_now)], axis=0)
        y_p = jnp.dot(products, band_2[...], preferred_element_type=F32)
        ybuf[0] = y_m[:, :LANES].reshape(group, ROWS, LANES)
        ybuf[1] = y_p[: group * ROWS].reshape(group, ROWS, LANES)
        ybuf[2] = y_p[group * ROWS :].reshape(group, ROWS, LANES)
        grad_y[at] = y_m[:, LANES:].reshape(group, ROWS, LANES)
        for j in range(group):
            for q in range(3):
                zbox[q, step * group + j] = z_sum(ybuf, q, j)

    @pl.loop(0, FPLANES)
    def _(i):
        mean = x_sum(0, i) / count_box
        var = x_sum(1, i) / count_box - mean * mean + var_eps
        cov = x_sum(2, i) / count_box - f_mean[i] * mean
        inv = 1.0 / var
        slope = cov * inv
        center = m_ext[i + 2, 5 : 5 + FROWS, :]
        term = 2.0 * slope * f_inv[i] * (f_dev[i] - slope * (center - mean))
        region = jnp.where(i >= SMOOTH_RADIUS, 1, 0) + jnp.where(i >= SMOOTH_RADIUS + SIDE, 1, 0)
        term = jnp.where(mask_pl[region] > 0.5, term, 0.0)
        half = 0.5 * term
        forces[i, 0] = half * (
            m_ext[i + 3, 5 : 5 + FROWS, :] - m_ext[i + 1, 5 : 5 + FROWS, :]
        )
        forces[i, 1] = half * (
            m_ext[i + 2, 6 : 6 + FROWS, :] - m_ext[i + 2, 4 : 4 + FROWS, :]
        )
        forces[i, 2] = term * grad_y[i + 2, 5 : 5 + FROWS, :]

    @pl.loop(0, FPLANES // 2)
    def _(step):
        at = pl.ds(step * 2, 2)
        rows = forces[at].reshape(6 * FROWS, LANES).astype(BF16)
        both = jnp.dot(rows, band_s[...], preferred_element_type=F32)
        ysm[at] = (both[:, :LANES] + both[:, LANES:]).reshape(2, 3, FROWS, LANES)

    def bell_sum(load):
        total = taps[3] * load(3)
        for t in range(3):
            total = total + taps[t] * (load(t) + load(6 - t))
        return total

    @pl.loop(0, FPLANES)
    def _(i):
        for c in range(3):
            zsm[c, i] = bell_sum(lambda t: ysm[i, c, t : t + SIDE, :])

    def last_pass(x, top):
        square = jnp.zeros((SIDE, LANES), F32)
        for c in range(3):
            value = bell_sum(lambda t: zsm[c, x + t])
            out_ref[c, x] = value
            square = square + value * value
        return jnp.maximum(top, square)

    top = lax.fori_loop(0, SIDE, last_pass, jnp.zeros((SIDE, LANES), F32))
    top = jnp.max(top.reshape(4, 8, LANES), axis=0)

    def all_peak(top, n, slots, ssem, rsem, device):
        pk = pk_send.at[0 if slots is pk_blk else 1]
        pk[...] = top
        copies = []
        for d in range(1, n):
            copies.append(
                pltpu.make_async_remote_copy(
                    src_ref=pk,
                    dst_ref=slots.at[d],
                    send_sem=ssem.at[d],
                    recv_sem=rsem.at[d],
                    device_id=device(d),
                    device_id_type=MESH,
                )
            )
        for copy in copies:
            copy.start()
        for d, copy in enumerate(copies):
            copy.wait_recv()
            top = jnp.maximum(top, slots[d + 1])
        return top, copies

    top, blk_copies = all_peak(
        top, n_blk, pk_blk, pb_ssem, pb_rsem, lambda d: (me_s, (me_b + d) % n_blk)
    )
    top, slab_copies = all_peak(
        top, n_slab, pk_slab, ps_ssem, ps_rsem, lambda d: ((me_s + d) % n_slab, me_b)
    )
    peak = jnp.sqrt(jnp.max(top, axis=(0, 1), keepdims=True))
    scale_ref[...] = jnp.broadcast_to(step_length / (peak + peak_eps), (8, LANES))

    for e in range(1, chips):
        spread(e).wait_send()
    for e in range(chips):
        to_sibling(e).wait_send()
    finish_all(f_copies)
    finish_all(m_copies)
    for copy in blk_copies + slab_copies:
        copy.wait_send()


def per_device(
    n_slab,
    n_blk,
    fixed_image,
    moving_image,
    fetch_owner,
    fetch_block,
    fetch_count,
    interp_level,
    block_mask,
):
    chips = n_blk // 2
    vmem = pl.BlockSpec(memory_space=pltpu.VMEM)
    smem = pl.BlockSpec(memory_space=pltpu.SMEM)
    rim = lambda planes, rows, n: pltpu.VMEM((n, planes, rows, LANES), BF16)
    sems = lambda n: pltpu.SemaphoreType.DMA((n,))
    smoothed, scale = pl.pallas_call(
        functools.partial(kernel, n_slab, n_blk),
        out_shape=(
            jax.ShapeDtypeStruct((3, SIDE, SIDE, LANES), F32),
            jax.ShapeDtypeStruct((8, LANES), F32),
        ),
        in_specs=[vmem, vmem, smem, smem, smem, smem, smem],
        out_specs=(vmem, vmem),
        scratch_shapes=[
            pltpu.VMEM((n_blk, SIDE, SIDE, LANES), BF16),
            pltpu.VMEM((chips, 2 * LANES, 4 * LANES), BF16),
            pltpu.VMEM((SIDE * SIDE, 4 * LANES), F32),
            pltpu.VMEM((PLANES, ROWS, LANES), F32),
            pltpu.VMEM((PLANES, ROWS, LANES), F32),
            pltpu.VMEM((3, 7, ROWS, LANES), F32),
            pltpu.VMEM((3, PLANES, FROWS, LANES), F32),
            pltpu.VMEM((FPLANES, FROWS, LANES), F32),
            pltpu.VMEM((FPLANES, FROWS, LANES), F32),
            pltpu.VMEM((FPLANES, FROWS, LANES), F32),
            pltpu.VMEM((PLANES, ROWS, LANES), F32),
            pltpu.VMEM((FPLANES, 3, FROWS, LANES), F32),
            pltpu.VMEM((FPLANES, 3, FROWS, LANES), F32),
            pltpu.VMEM((3, FPLANES, SIDE, LANES), F32),
            pltpu.VMEM((3, FROWS, LANES), F32),
            pltpu.VMEM((LANES, 2 * LANES), BF16),
            pltpu.VMEM((2 * LANES, LANES), BF16),
            pltpu.VMEM((LANES, 2 * LANES), BF16),
            rim(HALO + 1, SIDE, 2),
            rim(HALO + 1, SIDE, 2),
            rim(HALO + 1, SIDE, 2),
            rim(HALO + 1, SIDE, 2),
            rim(HALO + 1, 16, 4),
            rim(HALO, SIDE, 2),
            rim(HALO, SIDE, 2),
            rim(HALO, SIDE, 2),
            rim(HALO, SIDE, 2),
            rim(HALO, 16, 4),
            pltpu.VMEM((2, 8, LANES), F32),
            pltpu.VMEM((n_blk, 8, LANES), F32),
            pltpu.VMEM((n_slab, 8, LANES), F32),
            sems(n_blk),
            sems(n_blk),
            sems(8),
            sems(8),
            sems(8),
            sems(8),
            sems(n_blk),
            sems(n_blk),
            sems(n_slab),
            sems(n_slab),
        ],
        compiler_params=pltpu.CompilerParams(
            collective_id=0, has_side_effects=True, vmem_limit_bytes=48 * 1024 * 1024
        ),
        name="syn_step",
    )(
        fixed_image,
        moving_image,
        fetch_owner,
        fetch_block,
        fetch_count,
        interp_level,
        block_mask,
    )
    return smoothed * scale[0, 0]


def solution(mesh):
    in_specs = (
        P("blk", "slab", None),
        P("blk", "slab", None),
        P("blk", "slab", None, None),
        P("blk", "slab", None, None),
        P("blk", "slab", None),
        P("blk", "slab", None, None, None),
        P("blk", "slab", None),
    )
    out_specs = P(None, "blk", "slab", None)
    return jax.shard_map(
        functools.partial(per_device, mesh.shape["slab"], mesh.shape["blk"]),
        mesh=mesh,
        in_specs=in_specs,
        out_specs=out_specs,
        check_vma=False,
    )
```

time: 148 us -> 57.9 us (0.39)
  Pallas kernels: 0 us -> 49.8 us
  blocking collectives: 44 us -> 0 us
  waiting for transfers between devices: 29.8 us -> 0 us
  other arithmetic: 31.1 us -> 1.99 us
  starting transfers between devices: 26.4 us -> 0 us
  local copies, waits for them, and re-layouts: 13.6 us -> 5.86 us
    pallas_call x0 -> x1, Pallas kernels: none -> 49.8 us  [per_device(): pl.pallas_call(functools.partial(kernel, n_slab, n_blk), out_shape=(jax.S...]
    pmax x1 -> x0, blocking collectives: 44 us -> none  [per_device(): peak_norm = lax.pmax(jnp.max(norms), ('slab', 'blk'))]
    ppermute x8 -> x0, starting transfers between devices: 17 us -> none  [the longest x4 11.4 us: padded_2(): lax.ppermute(tail, axis, [(i, (i + 1) % count) for i in range(ends)])]
    add x13 -> x0, other arithmetic: 16 us -> none  [the longest x11 15.1 us: window_sum(): result + weights[offset] * lax.slice_in_dim(volume, offset, offset + leng...]
    all_to_all x2 -> x0, waiting for transfers between devices: 15.3 us -> none  [the longest x1 15.3 us: per_device(): lax.all_to_all(replies, 'blk', split_axis=0, concat_axis=0, tiled=True)]
    ppermute x8 -> x0, waiting for transfers between devices: 14.5 us -> none  [the longest x4 13.3 us: padded_2(): lax.ppermute(head, axis, [((i + 1) % count, i) for i in range(ends)])]
    all_to_all x2 -> x0, starting transfers between devices: 9.37 us -> none  [the longest x1 5.17 us: per_device(): lax.all_to_all(wanted, 'blk', split_axis=0, concat_axis=0, tiled=True)]
    reshape x6 -> x0, local copies, waits for them, and re-layouts: 6.24 us -> none  [the longest x1 2.05 us: per_device(): moving_image.reshape(block_side, block_side, blocks_dev, block_side)]
  transfers between devices with their start and end apart: 10 -> 0, of which waited for: 7 -> 0; matrix products, arithmetic and copies ran while one was open for 3% -> 0% of each run, Pallas kernels for 0% -> 0%
where the time goes in v1:
time: 57.9 us; the launch traced here: 57.7 us
  Pallas kernels  49.8 us (86%)
  local copies, waits for them, and re-layouts  5.86 us (10%)
  other arithmetic  1.99 us (3%)
    pallas_call x1, Pallas kernels, per_device(): pl.pallas_call(functools.partial(kernel, n_slab, n_blk), out_shape=(jax.S...  49.8 us
    unnamed x13, local copies, waits for them, and re-layouts  5.26 us
    mul x1, other arithmetic, per_device(): return smoothed * scale[0, 0]  1.99 us

profile of v1, /device:TPU:0, one launch (start us, length us, event | category | flops | bytes accessed | tf_op | source)
XLA Modules:
  0.0 57.7 jit_solution(2370433608178319973)
XLA Ops:
  0.0 0.7 %copy.8.level_ref = s32[1,1,4,3,4]{4,3,2,1,0:T(4,128)S(1)} copy(s32[1,1,4,3,4]{4,2,3,1,0:T(4,128)} %param.12) | data formatting | bytes 384 | tf_op args[5]
  0.7 0.0 copy-start
  0.7 0.9 %copy-done = bf16[32,32,128]{2,1,0:T(8,128)(2,1)S(1)} copy-done((bf16[32,32,128]{2,1,0:T(8,128)(2,1)S(1)}, bf16[32,32,128]{2,1,0:T(8,128)(2,1)}, u32[]{:S(2)}) %copy-start) | copy-done | bytes 262168
  1.6 0.0 copy-start.1
  1.6 0.9 %copy-done.1 = bf16[32,32,128]{2,1,0:T(8,128)(2,1)S(1)} copy-done((bf16[32,32,128]{2,1,0:T(8,128)(2,1)S(1)}, bf16[32,32,128]{2,1,0:T(8,128)(2,1)}, u32[]{:S(2)}) %copy-start.1) | copy-done | bytes 262168
  2.6 0.0 copy-start.2
  2.6 0.7 %copy-done.2 = s32[1,1,4,4]{3,2,1,0:T(4,128)S(1)} copy-done((s32[1,1,4,4]{3,2,1,0:T(4,128)S(1)}, s32[1,1,4,4]{3,2,1,0:T(4,128)}, u32[]{:S(2)}) %copy-start.2) | copy-done | bytes 88
  3.3 0.0 copy-start.3
  3.3 0.7 %copy-done.3 = s32[1,1,4,4]{3,2,1,0:T(4,128)S(1)} copy-done((s32[1,1,4,4]{3,2,1,0:T(4,128)S(1)}, s32[1,1,4,4]{3,2,1,0:T(4,128)}, u32[]{:S(2)}) %copy-start.3) | copy-done | bytes 88
  4.0 0.0 copy-start.4
  4.0 0.7 %copy-done.4 = s32[1,1,4]{2,1,0:T(1,128)S(1)} copy-done((s32[1,1,4]{2,1,0:T(1,128)S(1)}, s32[1,1,4]{2,1,0:T(1,128)}, u32[]{:S(2)}) %copy-start.4) | copy-done | bytes 40
  4.6 0.0 copy-start.5
  4.6 0.7 %copy-done.5 = s32[1,1,4]{2,1,0:T(1,128)S(1)} copy-done((s32[1,1,4]{2,1,0:T(1,128)S(1)}, s32[1,1,4]{2,1,0:T(1,128)}, u32[]{:S(2)}) %copy-start.5) | copy-done | bytes 40
  5.3 49.8 %syn_step.1 = (f32[3,32,32,128]{3,2,1,0:T(8,128)S(1)}, f32[8,128]{1,0:T(8,128)S(1)}) custom-call(bf16[32,32,128]{2,1,0:T(8,128)(2,1)S(1)} %copy-done, bf16[32,32,128]{2,1,0:T(8,128)(2,1)S(1)} %copy-done.1, s32[1,1,4,4]{3,2,1,0:T(4,128)S(1)} %copy-done.2, s32[1,1,4,4]{3,2,1,0:T(4,128)S(1)} %copy-done.3, s32[1,1,4]{2,1,0:T(1,128)S(1)} %copy-done.4, ...), custom_call_target="tpu_custom_call" | custom-call | tf_op jit(solution)/shard_map/syn_step/pallas_call | solution.py:511
  55.1 0.6 %slice.3 = f32[1,1]{1,0:T(1,128)} slice(f32[8,128]{1,0:T(8,128)S(1)} %get-tuple-element.8), slice={[0:1], [0:1]} | slice | bytes 8 | tf_op jit(solution)/shard_map/slice | solution.py:575
  55.7 2.0 %broadcast_multiply_fusion = f32[3,32,32,128]{3,2,1,0:T(8,128)} fusion(f32[3,32,32,128]{3,2,1,0:T(8,128)S(1)} %get-tuple-element.7, f32[]{:T(128)} %bitcast), kind=kLoop, calls=%fused_computation | loop fusion | flops 393216 | bytes 3145732 | tf_op jit(solution)/shard_map/mul | solution.py:575
Async XLA Ops:
  0.7 0.9 %copy-start = (bf16[32,32,128]{2,1,0:T(8,128)(2,1)S(1)}, bf16[32,32,128]{2,1,0:T(8,128)(2,1)}, u32[]{:S(2)}) copy-start(bf16[32,32,128]{2,1,0:T(8,128)(2,1)} %fixed_ref.1) | copy-start | bytes 786436
  1.6 0.9 %copy-start.1 = (bf16[32,32,128]{2,1,0:T(8,128)(2,1)S(1)}, bf16[32,32,128]{2,1,0:T(8,128)(2,1)}, u32[]{:S(2)}) copy-start(bf16[32,32,128]{2,1,0:T(8,128)(2,1)} %moving_ref.1) | copy-start | bytes 786436
  2.6 0.7 %copy-start.2 = (s32[1,1,4,4]{3,2,1,0:T(4,128)S(1)}, s32[1,1,4,4]{3,2,1,0:T(4,128)}, u32[]{:S(2)}) copy-start(s32[1,1,4,4]{3,2,1,0:T(4,128)} %owner_ref.1) | copy-start | bytes 196
  3.3 0.7 %copy-start.3 = (s32[1,1,4,4]{3,2,1,0:T(4,128)S(1)}, s32[1,1,4,4]{3,2,1,0:T(4,128)}, u32[]{:S(2)}) copy-start(s32[1,1,4,4]{3,2,1,0:T(4,128)} %block_ref.1) | copy-start | bytes 196
  4.0 0.7 %copy-start.4 = (s32[1,1,4]{2,1,0:T(1,128)S(1)}, s32[1,1,4]{2,1,0:T(1,128)}, u32[]{:S(2)}) copy-start(s32[1,1,4]{2,1,0:T(1,128)} %count_ref.1) | copy-start | bytes 52
  4.6 0.7 %copy-start.5 = (s32[1,1,4]{2,1,0:T(1,128)S(1)}, s32[1,1,4]{2,1,0:T(1,128)}, u32[]{:S(2)}) copy-start(s32[1,1,4]{2,1,0:T(1,128)} %mask_ref.1) | copy-start | bytes 52

commit v2 on v1

--- a/solution.py
+++ b/solution.py
@@ -43,21 +43,28 @@
 def kernel(
     n_slab,
     n_blk,
+    fixed_hbm,
+    moving_hbm,
+    owner_hbm,
+    block_hbm,
+    count_hbm,
+    level_hbm,
+    mask_hbm,
+    out_ref,
+    scale_ref,
     fixed_ref,
-    moving_ref,
     owner_ref,
     block_ref,
     count_ref,
     level_ref,
     mask_ref,
-    out_ref,
-    scale_ref,
+    in_sem,
     gath,
     select,
     acc,
     f_ext,
     m_ext,
-    ybuf,
+    ybox,
     zbox,
     f_mean,
     f_inv,
@@ -110,6 +117,23 @@
             ok = now if ok is None else jnp.logical_and(ok, now)
         return ok
 
+    loads = [
+        pltpu.make_async_copy(src, dst, in_sem.at[i])
+        for i, (src, dst) in enumerate(
+            (
+                (fixed_hbm, fixed_ref),
+                (moving_hbm, gath.at[0]),
+                (owner_hbm, owner_ref),
+                (block_hbm, block_ref),
+                (count_hbm, count_ref),
+                (level_hbm, level_ref),
+                (mask_hbm, mask_ref),
+            )
+        )
+    ]
+    for load in loads:
+        load.start()
+
     barrier = pltpu.get_barrier_semaphore()
     for d in range(1, n_blk):
         pl.semaphore_signal(
@@ -131,29 +155,60 @@
     wide_z = jnp.where(me_s > 0, 1, 0) + jnp.where(me_s < n_slab - 1, 1, 0)
     pl.semaphore_wait(barrier, n_blk - 1 + n_slab - 1 + wide_x * wide_z)
 
-    def spread(e):
+    if chips == 4:
+        flip_x = chip + 1 - 2 * (chip % 2)
+        flip_y = chip + 2 - 4 * (chip // 2)
+        away = [chip, flip_x, flip_y, 3 - chip]
+    else:
+        away = [(chip + chips - e) % chips for e in range(chips)]
+    half = SIDE // 2
+
+    def remote(src, dst, at, device):
         return pltpu.make_async_remote_copy(
-            src_ref=moving_ref,
-            dst_ref=gath.at[2 * e],
-            send_sem=ag_ssem.at[2 * e],
-            recv_sem=ag_rsem.at[2 * e],
-            device_id=(me_s, 2 * ((chip + e) % chips) + core),
+            src_ref=src,
+            dst_ref=dst,
+            send_sem=ag_ssem.at[at],
+            recv_sem=ag_rsem.at[at],
+            device_id=device,
             device_id_type=MESH,
         )
 
-    def to_sibling(e):
-        return pltpu.make_async_remote_copy(
-            src_ref=moving_ref if e == 0 else gath.at[2 * e],
-            dst_ref=gath.at[2 * e + 1],
-            send_sem=ag_ssem.at[2 * e + 1],
-            recv_sem=ag_rsem.at[2 * e + 1],
-            device_id=(me_s, 2 * chip + 1 - core),
-            device_id_type=MESH,
+    def piece(e, h):
+        rows = pl.ds(h * half, half)
+        at = 4 * e + 2 * h
+        if chips != 4:
+            target = (chip + e) % chips
+            src = moving_hbm.at[rows]
+        elif e < 3:
+            target = away[e]
+            src = moving_hbm.at[rows]
+        else:
+            target = away[2 - h]
+            src = gath.at[2 * (1 + h), rows]
+        return remote(src, gath.at[2 * e, rows], at, (me_s, 2 * target + core))
+
+    def passed(e, h):
+        rows = pl.ds(h * half, half)
+        src = moving_hbm.at[rows] if e == 0 else gath.at[2 * e, rows]
+        return remote(
+            src, gath.at[2 * e + 1, rows], 4 * e + 2 * h + 1, (me_s, 2 * chip + 1 - core)
         )
 
-    for e in range(1, chips):
-        spread(e).start()
-    to_sibling(0).start()
+    if chips == 4:
+        for e, h in ((1, 0), (2, 1), (1, 1), (2, 0)):
+            piece(e, h).start()
+    else:
+        for e in range(1, chips):
+            for h in range(2):
+                piece(e, h).start()
+    for h in range(2):
+        passed(0, h).start()
+
+    def take(e, h):
+        piece(e, h).wait_recv()
+        if chips == 4 and (e, h) in ((1, 0), (2, 1)):
+            piece(3, h).start()
+        passed(e, h).start()
 
     def rim_copies(x_send, z_send, x_recv, z_recv, c_recv, ssem, rsem):
         copies = []
@@ -235,20 +290,25 @@
             vec = jnp.where(lane // SIDE == g, scalars[g], vec)
         return vec
 
+    nought = me_b // n_blk
     for ext in (f_ext, m_ext):
 
-        @pl.loop(0, PLANES)
+        @pl.loop(0, PLANES // 7)
         def _(x):
-            ext[x] = jnp.zeros((ROWS, LANES), F32)
+            ext[pl.ds(x * 7, 7)] = jnp.zeros((7, ROWS, LANES), F32)
+
+    for load in loads:
+        load.wait()
 
     mask_pl[...] = jnp.zeros_like(mask_pl)
     own_mask = by_block([mask_ref[0, 0, g] for g in range(4)]).astype(F32)
     mask_rows = jnp.broadcast_to(own_mask, (SIDE, LANES))
     mask_pl[1, SMOOTH_RADIUS : SMOOTH_RADIUS + SIDE, :] = mask_rows
 
-    @pl.loop(0, SIDE)
+    @pl.loop(0, SIDE // 4)
     def _(x):
-        f_ext[HALO + x, FIRST : FIRST + SIDE, :] = fixed_ref[x].astype(F32)
+        at = pl.ds(HALO + x * 4, 4)
+        f_ext[at, FIRST : FIRST + SIDE, :] = fixed_ref[pl.ds(x * 4, 4)].astype(F32)
 
     pack_rims(f_ext, fx_send, fz_send)
     for side in range(2):
@@ -261,7 +321,7 @@
     counts = by_block([count_ref[0, 0, g] for g in range(4)])
     for k in range(4):
         fracs = [
-            by_block([level_ref[0, 0, g, a, k] for g in range(4)]).astype(F32) / LEVELS
+            by_block([level_ref[0, 0, a, g, k] for g in range(4)]).astype(F32) / LEVELS
             for a in range(3)
         ]
         frac_x.append(fracs[0])
@@ -276,7 +336,7 @@
     sub = lax.broadcasted_iota(jnp.int32, (LANES, LANES), 0)
     for e in range(chips):
         for p in range(2):
-            base = (2 * ((chip + chips - e) % chips) + (core if p == 0 else 1 - core)) * LANES
+            base = (2 * away[e] + (core if p == 0 else 1 - core)) * LANES
             for k in range(4):
                 first = place[k] - base
                 second = first + jnp.where(lane % SIDE == SIDE - 1, 0, 1)
@@ -304,53 +364,23 @@
         high = product.astype(BF16)
         return jnp.concatenate([high, (product - high.astype(F32)).astype(BF16)], axis=1)
 
+    def shifted(ref, lead, start, rows):
+        return ref[(*lead, pl.ds(nought + start, rows), slice(None))]
+
     def z_sum(ref, q, j):
-        total = ref[q, j, 3 : 3 + FROWS, :]
+        total = shifted(ref, (q, j), 3, FROWS)
         for t in range(1, 5):
-            total = total + ref[q, j, 3 + t : 3 + t + FROWS, :]
+            total = total + shifted(ref, (q, j), 3 + t, FROWS)
         return total
 
-    def x_sum(q, i):
-        total = zbox[q, i]
-        for t in range(1, 5):
-            total = total + zbox[q, i + t]
-        return total
-
-    count_box = float((2 * BOX_RADIUS + 1) ** 3)
-    group = 7
-
-    fill_rims(f_copies, f_ext, fx_recv, fz_recv, fc_recv, True)
-
-    @pl.loop(0, PLANES // group)
-    def _(step):
-        planes = f_ext[pl.ds(step * group, group)].reshape(group * ROWS, LANES)
-        y_f = jnp.dot(planes.astype(BF16), band, preferred_element_type=F32)
-        y_ff = jnp.dot(halves(planes * planes), band_2[...], preferred_element_type=F32)
-        ybuf[0] = y_f.reshape(group, ROWS, LANES)
-        ybuf[1] = y_ff.reshape(group, ROWS, LANES)
-        for j in range(group):
-            for q in range(2):
-                zbox[q, step * group + j] = z_sum(ybuf, q, j)
-
-    @pl.loop(0, FPLANES)
-    def _(i):
-        mean = x_sum(0, i) / count_box
-        var = x_sum(1, i) / count_box - mean * mean + var_eps
-        f_mean[i] = mean
-        f_inv[i] = 1.0 / var
-        f_dev[i] = f_ext[i + 2, 5 : 5 + FROWS, :] - mean
-
-    @pl.loop(0, SIDE)
-    def _(x):
-        gath[0, x] = moving_ref[x]
-
-    for e in range(chips):
-        if e > 0:
-            spread(e).wait_recv()
-            to_sibling(e).start()
-    for e in range(chips):
-        to_sibling(e).wait_recv()
-
+    def x_sums(q, i):
+        v = [zbox[q, i + t] for t in range(6)]
+        shared = (v[1] + v[2]) + (v[3] + v[4])
+        return v[0] + shared, shared + v[5]
+
+    per_box = 1.0 / float((2 * BOX_RADIUS + 1) ** 3)
+
+    def resample(e):
         @pl.loop(0, 4)
         def _(part):
             at = pl.ds(part * 8, 8)
@@ -365,9 +395,59 @@
             else:
                 acc[rows, :] = acc[rows, :] + got
 
+    if chips == 4:
+        take(1, 0)
+        take(2, 1)
+
+    fill_rims(f_copies, f_ext, fx_recv, fz_recv, fc_recv, True)
+
+    @pl.loop(0, PLANES // 7)
+    def _(step):
+        at = pl.ds(step * 7, 7)
+        planes = f_ext[at].reshape(7 * ROWS, LANES)
+        y_f = jnp.dot(planes.astype(BF16), band, preferred_element_type=F32)
+        y_ff = jnp.dot(halves(planes * planes), band_2[...], preferred_element_type=F32)
+        ybox[0, at] = y_f.reshape(7, ROWS, LANES)
+        ybox[1, at] = y_ff.reshape(7, ROWS, LANES)
+
+    if chips == 4:
+        take(1, 1)
+        take(2, 0)
+
+    @pl.loop(0, PLANES // 2)
+    def _(step):
+        for j in range(2):
+            for q in range(2):
+                zbox[q, 2 * step + j] = z_sum(ybox, q, 2 * step + j)
+
+    @pl.loop(0, FPLANES // 2)
+    def _(step):
+        i = 2 * step
+        sums = x_sums(0, i), x_sums(1, i)
+        for j in range(2):
+            mean = sums[0][j] * per_box
+            var = sums[1][j] * per_box - mean * mean + var_eps
+            f_mean[i + j] = mean
+            f_inv[i + j] = 1.0 / var
+            f_dev[i + j] = shifted(f_ext, (i + j + 2,), 5, FROWS) - mean
+
+    for h in range(2):
+        passed(0, h).wait_recv()
+    resample(0)
+    if chips != 4:
+        for e in range(1, chips):
+            for h in range(2):
+                take(e, h)
+    for e in range(1, chips):
+        for h in range(2):
+            if chips == 4 and e == 2:
+                take(3, h)
+            passed(e, h).wait_recv()
+        resample(e)
+
     last_row = lax.broadcasted_iota(jnp.int32, (SIDE, LANES), 0) == SIDE - 1
 
-    @pl.loop(0, SIDE)
+    @pl.loop(0, SIDE, unroll=2)
     def _(x):
         here = pl.ds(pl.multiple_of(x * SIDE, SIDE), SIDE)
         after = pl.ds(pl.multiple_of(jnp.minimum(x + 1, SIDE - 1) * SIDE, SIDE), SIDE)
@@ -384,71 +464,92 @@
     pack_rims(m_ext, mx_send, mz_send)
     m_copies = rim_copies(mx_send, mz_send, mx_recv, mz_recv, mc_recv, m_ssem, m_rsem)
     start_all(m_copies)
-    fill_rims(m_copies, m_ext, mx_recv, mz_recv, mc_recv, False)
-
-    @pl.loop(0, PLANES // group)
-    def _(step):
-        at = pl.ds(step * group, group)
-        m_now = m_ext[at].reshape(group * ROWS, LANES)
-        f_now = f_ext[at].reshape(group * ROWS, LANES)
+
+    def y_pass(planes, rows, shape):
+        count = shape[0] * shape[1]
+        m_now = m_ext[planes, rows].reshape(count, LANES)
+        f_now = f_ext[planes, rows].reshape(count, LANES)
         y_m = jnp.dot(m_now.astype(BF16), band_m[...], preferred_element_type=F32)
         products = jnp.concatenate([halves(m_now * m_now), halves(f_now * m_now)], axis=0)
         y_p = jnp.dot(products, band_2[...], preferred_element_type=F32)
-        ybuf[0] = y_m[:, :LANES].reshape(group, ROWS, LANES)
-        ybuf[1] = y_p[: group * ROWS].reshape(group, ROWS, LANES)
-        ybuf[2] = y_p[group * ROWS :].reshape(group, ROWS, LANES)
-        grad_y[at] = y_m[:, LANES:].reshape(group, ROWS, LANES)
-        for j in range(group):
+        ybox[0, planes, rows] = y_m[:, :LANES].reshape(*shape, LANES)
+        grad_y[planes, rows] = y_m[:, LANES:].reshape(*shape, LANES)
+        ybox[1, planes, rows] = y_p[:count].reshape(*shape, LANES)
+        ybox[2, planes, rows] = y_p[count:].reshape(*shape, LANES)
+
+    @pl.loop(0, 4)
+    def _(part):
+        y_pass(pl.ds(HALO + part * 8, 8), slice(FIRST, FIRST + SIDE), (8, SIDE))
+
+    fill_rims(m_copies, m_ext, mx_recv, mz_recv, mc_recv, False)
+    y_pass(slice(0, HALO), slice(None), (HALO, ROWS))
+    y_pass(slice(HALO + SIDE, PLANES), slice(None), (HALO, ROWS))
+    y_pass(slice(HALO, HALO + SIDE), slice(0, FIRST), (SIDE, FIRST))
+    y_pass(slice(HALO, HALO + SIDE), slice(FIRST + SIDE, ROWS), (SIDE, ROWS - FIRST - SIDE))
+
+    @pl.loop(0, PLANES // 2)
+    def _(step):
+        for j in range(2):
             for q in range(3):
-                zbox[q, step * group + j] = z_sum(ybuf, q, j)
-
-    @pl.loop(0, FPLANES)
-    def _(i):
-        mean = x_sum(0, i) / count_box
-        var = x_sum(1, i) / count_box - mean * mean + var_eps
-        cov = x_sum(2, i) / count_box - f_mean[i] * mean
-        inv = 1.0 / var
-        slope = cov * inv
-        center = m_ext[i + 2, 5 : 5 + FROWS, :]
-        term = 2.0 * slope * f_inv[i] * (f_dev[i] - slope * (center - mean))
-        region = jnp.where(i >= SMOOTH_RADIUS, 1, 0) + jnp.where(i >= SMOOTH_RADIUS + SIDE, 1, 0)
-        term = jnp.where(mask_pl[region] > 0.5, term, 0.0)
-        half = 0.5 * term
-        forces[i, 0] = half * (
-            m_ext[i + 3, 5 : 5 + FROWS, :] - m_ext[i + 1, 5 : 5 + FROWS, :]
-        )
-        forces[i, 1] = half * (
-            m_ext[i + 2, 6 : 6 + FROWS, :] - m_ext[i + 2, 4 : 4 + FROWS, :]
-        )
-        forces[i, 2] = term * grad_y[i + 2, 5 : 5 + FROWS, :]
-
-    @pl.loop(0, FPLANES // 2)
+                zbox[q, 2 * step + j] = z_sum(ybox, q, 2 * step + j)
+
+    def bell_sum(values):
+        total = taps[3] * values[3]
+        for t in range(3):
+            total = total + taps[t] * (values[t] + values[6 - t])
+        return total
+
+    pairs = FPLANES // 2
+
+    @pl.loop(0, pairs + 2)
     def _(step):
-        at = pl.ds(step * 2, 2)
-        rows = forces[at].reshape(6 * FROWS, LANES).astype(BF16)
-        both = jnp.dot(rows, band_s[...], preferred_element_type=F32)
-        ysm[at] = (both[:, :LANES] + both[:, LANES:]).reshape(2, 3, FROWS, LANES)
-
-    def bell_sum(load):
-        total = taps[3] * load(3)
-        for t in range(3):
-            total = total + taps[t] * (load(t) + load(6 - t))
-        return total
-
-    @pl.loop(0, FPLANES)
-    def _(i):
+        old = jnp.maximum(step - 2, 0)
+        for j in range(2):
+            for c in range(3):
+                zsm[c, 2 * old + j] = bell_sum(
+                    [shifted(ysm, (old, 3 * j + c), t, SIDE) for t in range(7)]
+                )
+        mid = jnp.minimum(jnp.maximum(step - 1, 0), pairs - 1)
+        both = jnp.dot(forces[mid].astype(BF16), band_s[...], preferred_element_type=F32)
+        ysm[mid] = (both[:, :LANES] + both[:, LANES:]).reshape(6, FROWS, LANES)
+        now = jnp.minimum(step, pairs - 1)
+        i = 2 * now
+        sums = [x_sums(q, i) for q in range(3)]
+        for j in range(2):
+            at = i + j
+            mean = sums[0][j] * per_box
+            var = sums[1][j] * per_box - mean * mean + var_eps
+            cov = sums[2][j] * per_box - f_mean[at] * mean
+            slope = cov / var
+            center = shifted(m_ext, (at + 2,), 5, FROWS)
+            term = slope * f_inv[at] * (f_dev[at] - slope * (center - mean))
+            region = jnp.where(at >= SMOOTH_RADIUS, 1, 0) + jnp.where(
+                at >= SMOOTH_RADIUS + SIDE, 1, 0
+            )
+            term = jnp.where(mask_pl[region] > 0.5, term, 0.0)
+            base = 3 * j * FROWS
+            forces[now, base : base + FROWS] = term * (
+                shifted(m_ext, (at + 3,), 5, FROWS) - shifted(m_ext, (at + 1,), 5, FROWS)
+            )
+            forces[now, base + FROWS : base + 2 * FROWS] = term * (
+                shifted(m_ext, (at + 2,), 6, FROWS) - shifted(m_ext, (at + 2,), 4, FROWS)
+            )
+            forces[now, base + 2 * FROWS : base + 3 * FROWS] = (
+                2.0 * term * shifted(grad_y, (at + 2,), 5, FROWS)
+            )
+
+    def last_pass(step, top):
+        x = 2 * step
+        squares = [jnp.zeros((SIDE, LANES), F32) for _ in range(2)]
         for c in range(3):
-            zsm[c, i] = bell_sum(lambda t: ysm[i, c, t : t + SIDE, :])
-
-    def last_pass(x, top):
-        square = jnp.zeros((SIDE, LANES), F32)
-        for c in range(3):
-            value = bell_sum(lambda t: zsm[c, x + t])
-            out_ref[c, x] = value
-            square = square + value * value
-        return jnp.maximum(top, square)
-
-    top = lax.fori_loop(0, SIDE, last_pass, jnp.zeros((SIDE, LANES), F32))
+            values = [zsm[c, x + t] for t in range(8)]
+            for j in range(2):
+                value = bell_sum(values[j : j + 7])
+                out_ref[c, x + j] = value
+                squares[j] = squares[j] + value * value
+        return jnp.maximum(top, jnp.maximum(squares[0], squares[1]))
+
+    top = lax.fori_loop(0, SIDE // 2, last_pass, jnp.zeros((SIDE, LANES), F32))
     top = jnp.max(top.reshape(4, 8, LANES), axis=0)
 
     def all_peak(top, n, slots, ssem, rsem, device):
@@ -480,12 +581,13 @@
         top, n_slab, pk_slab, ps_ssem, ps_rsem, lambda d: ((me_s + d) % n_slab, me_b)
     )
     peak = jnp.sqrt(jnp.max(top, axis=(0, 1), keepdims=True))
-    scale_ref[...] = jnp.broadcast_to(step_length / (peak + peak_eps), (8, LANES))
-
-    for e in range(1, chips):
-        spread(e).wait_send()
+    scale_ref[...] = jnp.broadcast_to(step_length / (peak + peak_eps), (1, LANES))
+
     for e in range(chips):
-        to_sibling(e).wait_send()
+        for h in range(2):
+            if e > 0:
+                piece(e, h).wait_send()
+            passed(e, h).wait_send()
     finish_all(f_copies)
     finish_all(m_copies)
     for copy in blk_copies + slab_copies:
@@ -504,32 +606,36 @@
     block_mask,
 ):
     chips = n_blk // 2
+    interp_level = jnp.swapaxes(interp_level, 2, 3)
     vmem = pl.BlockSpec(memory_space=pltpu.VMEM)
-    smem = pl.BlockSpec(memory_space=pltpu.SMEM)
+    small = [fetch_owner, fetch_block, fetch_count, interp_level, block_mask]
     rim = lambda planes, rows, n: pltpu.VMEM((n, planes, rows, LANES), BF16)
     sems = lambda n: pltpu.SemaphoreType.DMA((n,))
     smoothed, scale = pl.pallas_call(
         functools.partial(kernel, n_slab, n_blk),
         out_shape=(
             jax.ShapeDtypeStruct((3, SIDE, SIDE, LANES), F32),
-            jax.ShapeDtypeStruct((8, LANES), F32),
+            jax.ShapeDtypeStruct((1, LANES), F32),
         ),
-        in_specs=[vmem, vmem, smem, smem, smem, smem, smem],
+        in_specs=[pl.BlockSpec(memory_space=pl.ANY)] * 7,
         out_specs=(vmem, vmem),
         scratch_shapes=[
+            pltpu.VMEM((SIDE, SIDE, LANES), BF16),
+            *[pltpu.SMEM(one.shape, jnp.int32) for one in small],
+            sems(7),
             pltpu.VMEM((n_blk, SIDE, SIDE, LANES), BF16),
             pltpu.VMEM((chips, 2 * LANES, 4 * LANES), BF16),
             pltpu.VMEM((SIDE * SIDE, 4 * LANES), F32),
             pltpu.VMEM((PLANES, ROWS, LANES), F32),
             pltpu.VMEM((PLANES, ROWS, LANES), F32),
-            pltpu.VMEM((3, 7, ROWS, LANES), F32),
+            pltpu.VMEM((3, PLANES, ROWS, LANES), F32),
             pltpu.VMEM((3, PLANES, FROWS, LANES), F32),
             pltpu.VMEM((FPLANES, FROWS, LANES), F32),
             pltpu.VMEM((FPLANES, FROWS, LANES), F32),
             pltpu.VMEM((FPLANES, FROWS, LANES), F32),
             pltpu.VMEM((PLANES, ROWS, LANES), F32),
-            pltpu.VMEM((FPLANES, 3, FROWS, LANES), F32),
-            pltpu.VMEM((FPLANES, 3, FROWS, LANES), F32),
+            pltpu.VMEM((FPLANES // 2, 6 * FROWS, LANES), F32),
+            pltpu.VMEM((FPLANES // 2, 6, FROWS, LANES), F32),
             pltpu.VMEM((3, FPLANES, SIDE, LANES), F32),
             pltpu.VMEM((3, FROWS, LANES), F32),
             pltpu.VMEM((LANES, 2 * LANES), BF16),
@@ -548,8 +654,8 @@
             pltpu.VMEM((2, 8, LANES), F32),
             pltpu.VMEM((n_blk, 8, LANES), F32),
             pltpu.VMEM((n_slab, 8, LANES), F32),
-            sems(n_blk),
-            sems(n_blk),
+            sems(2 * n_blk),
+            sems(2 * n_blk),
             sems(8),
             sems(8),
             sems(8),
@@ -572,7 +678,7 @@
         interp_level,
         block_mask,
     )
-    return smoothed * scale[0, 0]
+    return smoothed * scale.reshape(1, 1, 1, LANES)
 
 
 def solution(mesh):

time: 57.9 us -> 48.6 us (0.84)
  Pallas kernels: 49.8 us -> 41.7 us
  other arithmetic: 1.99 us -> 1.3 us
  local copies, waits for them, and re-layouts: 5.86 us -> 5.26 us
    pallas_call x1, Pallas kernels: 49.8 us -> 41.7 us  [per_device(): pl.pallas_call(functools.partial(kernel, n_slab, n_blk), out_shape=(jax.S...]
    mul x1, other arithmetic: 1.99 us -> 1.3 us  [per_device(): return smoothed * scale.reshape(1, 1, 1, LANES)]
    slice x1 -> x0, local copies, waits for them, and re-layouts: 0.59 us -> none  [per_device(): return smoothed * scale[0, 0]]
    unnamed x13 -> x14, local copies, waits for them, and re-layouts: 5.26 us -> 5.26 us
where the time goes in v2:
time: 48.6 us; the launch traced here: 48.3 us
  Pallas kernels  41.7 us (86%)
  local copies, waits for them, and re-layouts  5.26 us (11%)
  other arithmetic  1.3 us (3%)
    pallas_call x1, Pallas kernels, per_device(): pl.pallas_call(functools.partial(kernel, n_slab, n_blk), out_shape=(jax.S...  41.7 us
    unnamed x14, local copies, waits for them, and re-layouts  5.26 us
    mul x1, other arithmetic, per_device(): return smoothed * scale.reshape(1, 1, 1, LANES)  1.3 us

profile of v2, /device:TPU:0, one launch (start us, length us, event | category | flops | bytes accessed | tf_op | source)
XLA Modules:
  0.0 48.3 jit_solution(14692771509952545464)
XLA Ops:
  0.0 0.0 copy-start
  0.0 0.9 %copy-done = bf16[32,32,128]{2,1,0:T(8,128)(2,1)S(1)} copy-done((bf16[32,32,128]{2,1,0:T(8,128)(2,1)S(1)}, bf16[32,32,128]{2,1,0:T(8,128)(2,1)}, u32[]{:S(2)}) %copy-start) | copy-done | bytes 262168
  1.0 0.0 copy-start.1
  1.0 0.9 %copy-done.1 = bf16[32,32,128]{2,1,0:T(8,128)(2,1)S(1)} copy-done((bf16[32,32,128]{2,1,0:T(8,128)(2,1)S(1)}, bf16[32,32,128]{2,1,0:T(8,128)(2,1)}, u32[]{:S(2)}) %copy-start.1) | copy-done | bytes 262168
  1.9 0.0 copy-start.2
  1.9 0.7 %copy-done.2 = s32[1,1,4,3,4]{4,2,3,1,0:T(4,128)S(1)} copy-done((s32[1,1,4,3,4]{4,2,3,1,0:T(4,128)S(1)}, s32[1,1,4,3,4]{4,2,3,1,0:T(4,128)}, u32[]{:S(2)}) %copy-start.2) | copy-done | bytes 216
  2.6 0.0 copy-start.3
  2.6 0.7 %copy-done.3 = s32[1,1,4,4]{3,2,1,0:T(4,128)S(1)} copy-done((s32[1,1,4,4]{3,2,1,0:T(4,128)S(1)}, s32[1,1,4,4]{3,2,1,0:T(4,128)}, u32[]{:S(2)}) %copy-start.3) | copy-done | bytes 88
  3.3 0.0 copy-start.4
  3.3 0.7 %copy-done.4 = s32[1,1,4,4]{3,2,1,0:T(4,128)S(1)} copy-done((s32[1,1,4,4]{3,2,1,0:T(4,128)S(1)}, s32[1,1,4,4]{3,2,1,0:T(4,128)}, u32[]{:S(2)}) %copy-start.4) | copy-done | bytes 88
  4.0 0.0 copy-start.5
  4.0 0.7 %copy-done.5 = s32[1,1,4]{2,1,0:T(1,128)S(1)} copy-done((s32[1,1,4]{2,1,0:T(1,128)S(1)}, s32[1,1,4]{2,1,0:T(1,128)}, u32[]{:S(2)}) %copy-start.5) | copy-done | bytes 40
  4.6 0.0 copy-start.6
  4.6 0.7 %copy-done.6 = s32[1,1,4]{2,1,0:T(1,128)S(1)} copy-done((s32[1,1,4]{2,1,0:T(1,128)S(1)}, s32[1,1,4]{2,1,0:T(1,128)}, u32[]{:S(2)}) %copy-start.6) | copy-done | bytes 40
  5.3 41.7 %syn_step.1 = (f32[3,32,32,128]{3,2,1,0:T(8,128)S(1)}, f32[1,128]{1,0:T(1,128)S(1)}) custom-call(bf16[32,32,128]{2,1,0:T(8,128)(2,1)S(1)} %copy-done, bf16[32,32,128]{2,1,0:T(8,128)(2,1)S(1)} %copy-done.1, s32[1,1,4,4]{3,2,1,0:T(4,128)S(1)} %copy-done.3, s32[1,1,4,4]{3,2,1,0:T(4,128)S(1)} %copy-done.4, s32[1,1,4]{2,1,0:T(1,128)S(1)} %copy-done.5, ...), custom_call_target="tpu_custom_call" | custom-call | tf_op jit(solution)/shard_map/syn_step/pallas_call | solution.py:614
  47.0 1.3 %broadcast_multiply_fusion = f32[3,32,32,128]{3,2,1,0:T(8,128)} fusion(f32[3,32,32,128]{3,2,1,0:T(8,128)S(1)} %get-tuple-element.7, f32[128]{0:T(128)S(1)} %bitcast.3), kind=kLoop, calls=%fused_computation | loop fusion | flops 393216 | bytes 3146240 | tf_op jit(solution)/shard_map/mul | solution.py:681
Async XLA Ops:
  0.0 0.9 %copy-start = (bf16[32,32,128]{2,1,0:T(8,128)(2,1)S(1)}, bf16[32,32,128]{2,1,0:T(8,128)(2,1)}, u32[]{:S(2)}) copy-start(bf16[32,32,128]{2,1,0:T(8,128)(2,1)} %fixed_hbm.1) | copy-start | bytes 786436
  1.0 0.9 %copy-start.1 = (bf16[32,32,128]{2,1,0:T(8,128)(2,1)S(1)}, bf16[32,32,128]{2,1,0:T(8,128)(2,1)}, u32[]{:S(2)}) copy-start(bf16[32,32,128]{2,1,0:T(8,128)(2,1)} %moving_hbm.1) | copy-start | bytes 786436
  1.9 0.7 %copy-start.2 = (s32[1,1,4,3,4]{4,2,3,1,0:T(4,128)S(1)}, s32[1,1,4,3,4]{4,2,3,1,0:T(4,128)}, u32[]{:S(2)}) copy-start(s32[1,1,4,3,4]{4,2,3,1,0:T(4,128)} %param.12) | copy-start | bytes 580
  2.6 0.7 %copy-start.3 = (s32[1,1,4,4]{3,2,1,0:T(4,128)S(1)}, s32[1,1,4,4]{3,2,1,0:T(4,128)}, u32[]{:S(2)}) copy-start(s32[1,1,4,4]{3,2,1,0:T(4,128)} %owner_hbm.1) | copy-start | bytes 196
  3.3 0.7 %copy-start.4 = (s32[1,1,4,4]{3,2,1,0:T(4,128)S(1)}, s32[1,1,4,4]{3,2,1,0:T(4,128)}, u32[]{:S(2)}) copy-start(s32[1,1,4,4]{3,2,1,0:T(4,128)} %block_hbm.1) | copy-start | bytes 196
  4.0 0.7 %copy-start.5 = (s32[1,1,4]{2,1,0:T(1,128)S(1)}, s32[1,1,4]{2,1,0:T(1,128)}, u32[]{:S(2)}) copy-start(s32[1,1,4]{2,1,0:T(1,128)} %count_hbm.1) | copy-start | bytes 52
  4.6 0.7 %copy-start.6 = (s32[1,1,4]{2,1,0:T(1,128)S(1)}, s32[1,1,4]{2,1,0:T(1,128)}, u32[]{:S(2)}) copy-start(s32[1,1,4]{2,1,0:T(1,128)} %mask_hbm.1) | copy-start | bytes 52

commit v3 on v2

--- a/solution.py
+++ b/solution.py
@@ -50,8 +50,10 @@
     count_hbm,
     level_hbm,
     mask_hbm,
+    out_hbm,
+    scale_ref,
     out_ref,
-    scale_ref,
+    out_sem,
     fixed_ref,
     owner_ref,
     block_ref,
@@ -151,65 +153,6 @@
                 barrier, inc=1, device_id=(me_s + dz, me_b + dx), device_id_type=MESH
             )
 
-    wide_x = jnp.where(me_b > 0, 1, 0) + jnp.where(me_b < n_blk - 1, 1, 0)
-    wide_z = jnp.where(me_s > 0, 1, 0) + jnp.where(me_s < n_slab - 1, 1, 0)
-    pl.semaphore_wait(barrier, n_blk - 1 + n_slab - 1 + wide_x * wide_z)
-
-    if chips == 4:
-        flip_x = chip + 1 - 2 * (chip % 2)
-        flip_y = chip + 2 - 4 * (chip // 2)
-        away = [chip, flip_x, flip_y, 3 - chip]
-    else:
-        away = [(chip + chips - e) % chips for e in range(chips)]
-    half = SIDE // 2
-
-    def remote(src, dst, at, device):
-        return pltpu.make_async_remote_copy(
-            src_ref=src,
-            dst_ref=dst,
-            send_sem=ag_ssem.at[at],
-            recv_sem=ag_rsem.at[at],
-            device_id=device,
-            device_id_type=MESH,
-        )
-
-    def piece(e, h):
-        rows = pl.ds(h * half, half)
-        at = 4 * e + 2 * h
-        if chips != 4:
-            target = (chip + e) % chips
-            src = moving_hbm.at[rows]
-        elif e < 3:
-            target = away[e]
-            src = moving_hbm.at[rows]
-        else:
-            target = away[2 - h]
-            src = gath.at[2 * (1 + h), rows]
-        return remote(src, gath.at[2 * e, rows], at, (me_s, 2 * target + core))
-
-    def passed(e, h):
-        rows = pl.ds(h * half, half)
-        src = moving_hbm.at[rows] if e == 0 else gath.at[2 * e, rows]
-        return remote(
-            src, gath.at[2 * e + 1, rows], 4 * e + 2 * h + 1, (me_s, 2 * chip + 1 - core)
-        )
-
-    if chips == 4:
-        for e, h in ((1, 0), (2, 1), (1, 1), (2, 0)):
-            piece(e, h).start()
-    else:
-        for e in range(1, chips):
-            for h in range(2):
-                piece(e, h).start()
-    for h in range(2):
-        passed(0, h).start()
-
-    def take(e, h):
-        piece(e, h).wait_recv()
-        if chips == 4 and (e, h) in ((1, 0), (2, 1)):
-            piece(3, h).start()
-        passed(e, h).start()
-
     def rim_copies(x_send, z_send, x_recv, z_recv, c_recv, ssem, rsem):
         copies = []
         for i, (dx, dz) in enumerate(DIRECTIONS):
@@ -297,8 +240,8 @@
         def _(x):
             ext[pl.ds(x * 7, 7)] = jnp.zeros((7, ROWS, LANES), F32)
 
-    for load in loads:
-        load.wait()
+    loads[0].wait()
+    loads[6].wait()
 
     mask_pl[...] = jnp.zeros_like(mask_pl)
     own_mask = by_block([mask_ref[0, 0, g] for g in range(4)]).astype(F32)
@@ -314,36 +257,120 @@
     for side in range(2):
         fx_send[side, HALO] = mask_rows.astype(BF16)
         fz_send[side, HALO] = mask_rows.astype(BF16)
+    wide_x = jnp.where(me_b > 0, 1, 0) + jnp.where(me_b < n_blk - 1, 1, 0)
+    wide_z = jnp.where(me_s > 0, 1, 0) + jnp.where(me_s < n_slab - 1, 1, 0)
+    pl.semaphore_wait(barrier, n_blk - 1 + n_slab - 1 + wide_x * wide_z)
+
     f_copies = rim_copies(fx_send, fz_send, fx_recv, fz_recv, fc_recv, f_ssem, f_rsem)
     start_all(f_copies)
 
-    place, frac_x, frac_y, frac_z, weight = [], [], [], [], []
+    if chips == 4:
+        flip_x = chip + 1 - 2 * (chip % 2)
+        flip_y = chip + 2 - 4 * (chip // 2)
+        away = [chip, flip_x, flip_y, 3 - chip]
+    else:
+        away = [(chip + chips - e) % chips for e in range(chips)]
+    half = SIDE // 2
+
+    def remote(src, dst, at, device):
+        return pltpu.make_async_remote_copy(
+            src_ref=src,
+            dst_ref=dst,
+            send_sem=ag_ssem.at[at],
+            recv_sem=ag_rsem.at[at],
+            device_id=device,
+            device_id_type=MESH,
+        )
+
+    def piece(e, h):
+        rows = pl.ds(h * half, half)
+        at = 4 * e + 2 * h
+        if chips != 4:
+            target = (chip + e) % chips
+            src = moving_hbm.at[rows]
+        elif e < 3:
+            target = away[e]
+            src = moving_hbm.at[rows]
+        else:
+            target = away[2 - h]
+            src = gath.at[2 * (1 + h), rows]
+        return remote(src, gath.at[2 * e, rows], at, (me_s, 2 * target + core))
+
+    def passed(e, h):
+        rows = pl.ds(h * half, half)
+        src = moving_hbm.at[rows] if e == 0 else gath.at[2 * e, rows]
+        return remote(
+            src, gath.at[2 * e + 1, rows], 4 * e + 2 * h + 1, (me_s, 2 * chip + 1 - core)
+        )
+
+    if chips == 4:
+        for e, h in ((1, 0), (2, 1), (1, 1), (2, 0)):
+            piece(e, h).start()
+    else:
+        for e in range(1, chips):
+            for h in range(2):
+                piece(e, h).start()
+    for h in range(2):
+        passed(0, h).start()
+
+    def take(e, h):
+        piece(e, h).wait_recv()
+        if chips == 4 and (e, h) in ((1, 0), (2, 1)):
+            piece(3, h).start()
+        passed(e, h).start()
+
+    for load in loads[2:6]:
+        load.wait()
+    places, mixes = [], []
     counts = by_block([count_ref[0, 0, g] for g in range(4)])
+    at_end = lane % SIDE == SIDE - 1
     for k in range(4):
-        fracs = [
+        f_x, f_z, f_y = [
             by_block([level_ref[0, 0, a, g, k] for g in range(4)]).astype(F32) / LEVELS
             for a in range(3)
         ]
-        frac_x.append(fracs[0])
-        frac_z.append(fracs[1])
-        frac_y.append(fracs[2])
-        place.append(
+        places.append(
             by_block([owner_ref[0, 0, g, k] for g in range(4)]) * LANES
             + by_block([block_ref[0, 0, g, k] for g in range(4)]) * SIDE
             + lane % SIDE
         )
-        weight.append(jnp.where(counts > k, 1.0, 0.0) / counts.astype(F32))
+        listed = jnp.where(counts > k, 1.0, 0.0)
+        mixes.append(
+            (
+                jnp.where(at_end, 1.0, 1.0 - f_y),
+                jnp.where(at_end, 0.0, f_y),
+                [
+                    listed * (f_x if mx else 1.0 - f_x) * (f_z if mz else 1.0 - f_z)
+                    for mx, mz in ((0, 0), (1, 0), (0, 1), (1, 1))
+                ],
+            )
+        )
+    share = 1.0 / counts.astype(F32)
     sub = lax.broadcasted_iota(jnp.int32, (LANES, LANES), 0)
-    for e in range(chips):
-        for p in range(2):
-            base = (2 * away[e] + (core if p == 0 else 1 - core)) * LANES
-            for k in range(4):
-                first = place[k] - base
-                second = first + jnp.where(lane % SIDE == SIDE - 1, 0, 1)
-                f_y = frac_y[k]
-                select[e, p * LANES : (p + 1) * LANES, k * LANES : (k + 1) * LANES] = (
-                    jnp.where(sub == first, 1.0 - f_y, 0.0) + jnp.where(sub == second, f_y, 0.0)
-                ).astype(BF16)
+
+    @pl.loop(0, LANES // SIDE)
+    def _(part):
+        row = lax.broadcasted_iota(jnp.int32, (SIDE, LANES), 0) + part * SIDE
+        for e in range(chips):
+            for p in range(2):
+                base = (2 * away[e] + (core if p == 0 else 1 - core)) * LANES
+                totals = [None] * 4
+                for k in range(4):
+                    first = places[k] - base
+                    y_stay, y_move, mix = mixes[k]
+                    taken = jnp.where(
+                        row == first, y_stay, jnp.where(row == first + 1, y_move, 0.0)
+                    )
+                    for c in range(4):
+                        term = taken * mix[c]
+                        totals[c] = term if k == 0 else totals[c] + term
+                for c in range(4):
+                    cols = slice(c * LANES, (c + 1) * LANES)
+                    high = totals[c].astype(BF16)
+                    low = (totals[c] - high.astype(F32)).astype(BF16)
+                    at = pl.multiple_of(p * LANES + part * SIDE, SIDE)
+                    select[e, pl.ds(at, SIDE), cols] = high
+                    select[e, pl.ds(at + 2 * LANES, SIDE), cols] = low
 
     off = sub - lax.broadcasted_iota(jnp.int32, (LANES, LANES), 1)
     band = jnp.where(jnp.abs(off) <= BOX_RADIUS, 1.0, 0.0).astype(BF16)
@@ -378,6 +405,10 @@
         shared = (v[1] + v[2]) + (v[3] + v[4])
         return v[0] + shared, shared + v[5]
 
+    def inverse(value):
+        guess = pltpu.reciprocal(value, approx=True)
+        return guess * (2.0 - value * guess)
+
     per_box = 1.0 / float((2 * BOX_RADIUS + 1) ** 3)
 
     def resample(e):
@@ -388,6 +419,7 @@
                 [gath[2 * e, at].reshape(256, LANES), gath[2 * e + 1, at].reshape(256, LANES)],
                 axis=1,
             )
+            pair = jnp.concatenate([pair, pair], axis=1)
             got = jnp.dot(pair, select[e], preferred_element_type=F32)
             rows = pl.ds(part * 256, 256)
             if e == 0:
@@ -420,6 +452,11 @@
             for q in range(2):
                 zbox[q, 2 * step + j] = z_sum(ybox, q, 2 * step + j)
 
+    loads[1].wait()
+    for h in range(2):
+        passed(0, h).wait_recv()
+    resample(0)
+
     @pl.loop(0, FPLANES // 2)
     def _(step):
         i = 2 * step
@@ -428,12 +465,9 @@
             mean = sums[0][j] * per_box
             var = sums[1][j] * per_box - mean * mean + var_eps
             f_mean[i + j] = mean
-            f_inv[i + j] = 1.0 / var
+            f_inv[i + j] = inverse(var)
             f_dev[i + j] = shifted(f_ext, (i + j + 2,), 5, FROWS) - mean
 
-    for h in range(2):
-        passed(0, h).wait_recv()
-    resample(0)
     if chips != 4:
         for e in range(1, chips):
             for h in range(2):
@@ -447,19 +481,15 @@
 
     last_row = lax.broadcasted_iota(jnp.int32, (SIDE, LANES), 0) == SIDE - 1
 
-    @pl.loop(0, SIDE, unroll=2)
+    @pl.loop(0, SIDE, unroll=4)
     def _(x):
         here = pl.ds(pl.multiple_of(x * SIDE, SIDE), SIDE)
         after = pl.ds(pl.multiple_of(jnp.minimum(x + 1, SIDE - 1) * SIDE, SIDE), SIDE)
-        stay = jnp.zeros((SIDE, LANES), F32)
-        move = jnp.zeros((SIDE, LANES), F32)
-        for k in range(4):
-            cols = slice(k * LANES, (k + 1) * LANES)
-            mixed = (1.0 - frac_x[k]) * acc[here, cols] + frac_x[k] * acc[after, cols]
-            stay = stay + (weight[k] * (1.0 - frac_z[k])) * mixed
-            move = move + (weight[k] * frac_z[k]) * mixed
+        stay = acc[here, :LANES] + acc[after, LANES : 2 * LANES]
+        move = acc[here, 2 * LANES : 3 * LANES] + acc[after, 3 * LANES :]
         moved = jnp.where(last_row, move, pltpu.roll(move, SIDE - 1, 0))
-        m_ext[HALO + x, FIRST : FIRST + SIDE, :] = (stay + moved).astype(BF16).astype(F32)
+        warped = ((stay + moved) * share).astype(BF16).astype(F32)
+        m_ext[HALO + x, FIRST : FIRST + SIDE, :] = warped
 
     pack_rims(m_ext, mx_send, mz_send)
     m_copies = rim_copies(mx_send, mz_send, mx_recv, mz_recv, mc_recv, m_ssem, m_rsem)
@@ -520,7 +550,7 @@
             mean = sums[0][j] * per_box
             var = sums[1][j] * per_box - mean * mean + var_eps
             cov = sums[2][j] * per_box - f_mean[at] * mean
-            slope = cov / var
+            slope = cov * inverse(var)
             center = shifted(m_ext, (at + 2,), 5, FROWS)
             term = slope * f_inv[at] * (f_dev[at] - slope * (center - mean))
             region = jnp.where(at >= SMOOTH_RADIUS, 1, 0) + jnp.where(
@@ -551,6 +581,8 @@
 
     top = lax.fori_loop(0, SIDE // 2, last_pass, jnp.zeros((SIDE, LANES), F32))
     top = jnp.max(top.reshape(4, 8, LANES), axis=0)
+    write = pltpu.make_async_copy(out_ref, out_hbm, out_sem)
+    write.start()
 
     def all_peak(top, n, slots, ssem, rsem, device):
         pk = pk_send.at[0 if slots is pk_blk else 1]
@@ -588,6 +620,7 @@
             if e > 0:
                 piece(e, h).wait_send()
             passed(e, h).wait_send()
+    write.wait()
     finish_all(f_copies)
     finish_all(m_copies)
     for copy in blk_copies + slab_copies:
@@ -617,14 +650,16 @@
             jax.ShapeDtypeStruct((3, SIDE, SIDE, LANES), F32),
             jax.ShapeDtypeStruct((1, LANES), F32),
         ),
-        in_specs=[pl.BlockSpec(memory_space=pl.ANY)] * 7,
-        out_specs=(vmem, vmem),
+        in_specs=[pl.BlockSpec(memory_space=pltpu.HBM)] * 7,
+        out_specs=(pl.BlockSpec(memory_space=pltpu.HBM), vmem),
         scratch_shapes=[
+            pltpu.VMEM((3, SIDE, SIDE, LANES), F32),
+            pltpu.SemaphoreType.DMA,
             pltpu.VMEM((SIDE, SIDE, LANES), BF16),
             *[pltpu.SMEM(one.shape, jnp.int32) for one in small],
             sems(7),
             pltpu.VMEM((n_blk, SIDE, SIDE, LANES), BF16),
-            pltpu.VMEM((chips, 2 * LANES, 4 * LANES), BF16),
+            pltpu.VMEM((chips, 4 * LANES, 4 * LANES), BF16),
             pltpu.VMEM((SIDE * SIDE, 4 * LANES), F32),
             pltpu.VMEM((PLANES, ROWS, LANES), F32),
             pltpu.VMEM((PLANES, ROWS, LANES), F32),
@@ -666,7 +701,7 @@
             sems(n_slab),
         ],
         compiler_params=pltpu.CompilerParams(
-            collective_id=0, has_side_effects=True, vmem_limit_bytes=48 * 1024 * 1024
+            collective_id=0, has_side_effects=True, vmem_limit_bytes=64 * 1024 * 1024
         ),
         name="syn_step",
     )(

time: 48.6 us -> 43.1 us (0.89)
  local copies, waits for them, and re-layouts: 5.26 us -> 0 us
  Pallas kernels: 41.7 us -> 40.2 us
  other arithmetic: 1.3 us -> 2.75 us
    unnamed x14 -> x0, local copies, waits for them, and re-layouts: 5.26 us -> none
    pallas_call x1, Pallas kernels: 41.7 us -> 40.2 us  [per_device(): pl.pallas_call(functools.partial(kernel, n_slab, n_blk), out_shape=(jax.S...]
    mul x1, other arithmetic: 1.3 us -> 2.75 us  [per_device(): return smoothed * scale.reshape(1, 1, 1, LANES)]
where the time goes in v3:
time: 43.1 us; the launch traced here: 43 us
  Pallas kernels  40.2 us (93%)
  other arithmetic  2.75 us (6%)
    pallas_call x1, Pallas kernels, per_device(): pl.pallas_call(functools.partial(kernel, n_slab, n_blk), out_shape=(jax.S...  40.2 us
    mul x1, other arithmetic, per_device(): return smoothed * scale.reshape(1, 1, 1, LANES)  2.75 us

profile of v3, /device:TPU:0, one launch (start us, length us, event | category | flops | bytes accessed | tf_op | source)
XLA Modules:
  0.0 43.0 jit_solution(733850119861658599)
XLA Ops:
  0.0 40.2 %syn_step.1 = (f32[3,32,32,128]{3,2,1,0:T(8,128)}, f32[1,128]{1,0:T(1,128)}) custom-call(bf16[32,32,128]{2,1,0:T(8,128)(2,1)} %fixed_hbm.1, bf16[32,32,128]{2,1,0:T(8,128)(2,1)} %moving_hbm.1, s32[1,1,4,4]{3,2,1,0:T(4,128)} %owner_hbm.1, s32[1,1,4,4]{3,2,1,0:T(4,128)} %block_hbm.1, s32[1,1,4]{2,1,0:T(1,128)} %count_hbm.1, s32[1,1,3,4,4]{4,3,2,1,0:T(4,128)} %bitcast.2, ...), custom_call_target="tpu_custom_call" | custom-call | tf_op jit(solution)/shard_map/syn_step/pallas_call | solution.py:647
  40.2 2.8 %broadcast_multiply_fusion = f32[3,32,32,128]{3,2,1,0:T(8,128)} fusion(f32[3,32,32,128]{3,2,1,0:T(8,128)} %get-tuple-element.7, f32[128]{0:T(128)} %bitcast.3), kind=kLoop, calls=%fused_computation | loop fusion | flops 393216 | bytes 3146240 | tf_op jit(solution)/shard_map/mul | solution.py:716

commit v4 on v3

--- a/solution.py
+++ b/solution.py
@@ -394,14 +394,14 @@
     def shifted(ref, lead, start, rows):
         return ref[(*lead, pl.ds(nought + start, rows), slice(None))]
 
-    def z_sum(ref, q, j):
-        total = shifted(ref, (q, j), 3, FROWS)
+    def z_sum(q, j, first=0, rows=FROWS):
+        total = shifted(ybox, (q, j), first + 3, rows)
         for t in range(1, 5):
-            total = total + shifted(ref, (q, j), 3 + t, FROWS)
-        return total
-
-    def x_sums(q, i):
-        v = [zbox[q, i + t] for t in range(6)]
+            total = total + shifted(ybox, (q, j), first + 3 + t, rows)
+        zbox[q, j, first : first + rows] = total
+
+    def x_sums(q, i, first=0, rows=FROWS):
+        v = [zbox[q, i + t, first : first + rows] for t in range(6)]
         shared = (v[1] + v[2]) + (v[3] + v[4])
         return v[0] + shared, shared + v[5]
 
@@ -411,8 +411,8 @@
 
     per_box = 1.0 / float((2 * BOX_RADIUS + 1) ** 3)
 
-    def resample(e):
-        @pl.loop(0, 4)
+    def resample(e, begin=0, end=4):
+        @pl.loop(begin, end)
         def _(part):
             at = pl.ds(part * 8, 8)
             pair = jnp.concatenate(
@@ -450,7 +450,7 @@
     def _(step):
         for j in range(2):
             for q in range(2):
-                zbox[q, 2 * step + j] = z_sum(ybox, q, 2 * step + j)
+                z_sum(q, 2 * step + j)
 
     loads[1].wait()
     for h in range(2):
@@ -477,7 +477,10 @@
             if chips == 4 and e == 2:
                 take(3, h)
             passed(e, h).wait_recv()
-        resample(e)
+            if e == chips - 1:
+                resample(e, 2 * h, 2 * h + 2)
+        if e < chips - 1:
+            resample(e)
 
     last_row = lax.broadcasted_iota(jnp.int32, (SIDE, LANES), 0) == SIDE - 1
 
@@ -511,17 +514,65 @@
     def _(part):
         y_pass(pl.ds(HALO + part * 8, 8), slice(FIRST, FIRST + SIDE), (8, SIDE))
 
+    edge = 3
+    inner = slice(8, 32)
+    outer = (slice(0, 8), slice(32, FROWS))
+
+    def force_rows(now, rows):
+        first, n = rows.start, rows.stop - rows.start
+        i = 2 * now
+        sums = [x_sums(q, i, first, n) for q in range(3)]
+        for j in range(2):
+            at = i + j
+            mean = sums[0][j] * per_box
+            var = sums[1][j] * per_box - mean * mean + var_eps
+            cov = sums[2][j] * per_box - f_mean[at, rows] * mean
+            slope = cov * inverse(var)
+            center = shifted(m_ext, (at + 2,), 5 + first, n)
+            term = slope * f_inv[at, rows] * (f_dev[at, rows] - slope * (center - mean))
+            region = jnp.where(at >= SMOOTH_RADIUS, 1, 0) + jnp.where(
+                at >= SMOOTH_RADIUS + SIDE, 1, 0
+            )
+            term = jnp.where(mask_pl[region, rows] > 0.5, term, 0.0)
+            steps = (
+                shifted(m_ext, (at + 3,), 5 + first, n) - shifted(m_ext, (at + 1,), 5 + first, n),
+                shifted(m_ext, (at + 2,), 6 + first, n) - shifted(m_ext, (at + 2,), 4 + first, n),
+                2.0 * shifted(grad_y, (at + 2,), 5 + first, n),
+            )
+            for c in range(3):
+                base = (3 * j + c) * FROWS + first
+                forces[now, base : base + n] = term * steps[c]
+
+    @pl.loop(0, SIDE // 2)
+    def _(step):
+        for j in range(2):
+            for q in range(3):
+                z_sum(q, HALO + 2 * step + j, 8, 24)
+
+    pairs = FPLANES // 2
+
+    @pl.loop(edge, pairs - edge)
+    def _(now):
+        force_rows(now, inner)
+
     fill_rims(m_copies, m_ext, mx_recv, mz_recv, mc_recv, False)
     y_pass(slice(0, HALO), slice(None), (HALO, ROWS))
     y_pass(slice(HALO + SIDE, PLANES), slice(None), (HALO, ROWS))
     y_pass(slice(HALO, HALO + SIDE), slice(0, FIRST), (SIDE, FIRST))
     y_pass(slice(HALO, HALO + SIDE), slice(FIRST + SIDE, ROWS), (SIDE, ROWS - FIRST - SIDE))
 
-    @pl.loop(0, PLANES // 2)
+    @pl.loop(0, HALO)
     def _(step):
-        for j in range(2):
+        for at in (step, HALO + SIDE + step):
             for q in range(3):
-                zbox[q, 2 * step + j] = z_sum(ybox, q, 2 * step + j)
+                z_sum(q, at)
+
+    @pl.loop(0, SIDE // 4)
+    def _(step):
+        for j in range(4):
+            for q in range(3):
+                for rows in outer:
+                    z_sum(q, HALO + 4 * step + j, rows.start, 8)
 
     def bell_sum(values):
         total = taps[3] * values[3]
@@ -529,10 +580,7 @@
             total = total + taps[t] * (values[t] + values[6 - t])
         return total
 
-    pairs = FPLANES // 2
-
-    @pl.loop(0, pairs + 2)
-    def _(step):
+    def stages(step, row_sets):
         old = jnp.maximum(step - 2, 0)
         for j in range(2):
             for c in range(3):
@@ -542,31 +590,19 @@
         mid = jnp.minimum(jnp.maximum(step - 1, 0), pairs - 1)
         both = jnp.dot(forces[mid].astype(BF16), band_s[...], preferred_element_type=F32)
         ysm[mid] = (both[:, :LANES] + both[:, LANES:]).reshape(6, FROWS, LANES)
-        now = jnp.minimum(step, pairs - 1)
-        i = 2 * now
-        sums = [x_sums(q, i) for q in range(3)]
-        for j in range(2):
-            at = i + j
-            mean = sums[0][j] * per_box
-            var = sums[1][j] * per_box - mean * mean + var_eps
-            cov = sums[2][j] * per_box - f_mean[at] * mean
-            slope = cov * inverse(var)
-            center = shifted(m_ext, (at + 2,), 5, FROWS)
-            term = slope * f_inv[at] * (f_dev[at] - slope * (center - mean))
-            region = jnp.where(at >= SMOOTH_RADIUS, 1, 0) + jnp.where(
-                at >= SMOOTH_RADIUS + SIDE, 1, 0
-            )
-            term = jnp.where(mask_pl[region] > 0.5, term, 0.0)
-            base = 3 * j * FROWS
-            forces[now, base : base + FROWS] = term * (
-                shifted(m_ext, (at + 3,), 5, FROWS) - shifted(m_ext, (at + 1,), 5, FROWS)
-            )
-            forces[now, base + FROWS : base + 2 * FROWS] = term * (
-                shifted(m_ext, (at + 2,), 6, FROWS) - shifted(m_ext, (at + 2,), 4, FROWS)
-            )
-            forces[now, base + 2 * FROWS : base + 3 * FROWS] = (
-                2.0 * term * shifted(grad_y, (at + 2,), 5, FROWS)
-            )
+        for rows in row_sets:
+            force_rows(step, rows)
+
+    for begin, end, row_sets in (
+        (0, edge, (slice(0, FROWS),)),
+        (edge, pairs - edge, outer),
+        (pairs - edge, pairs, (slice(0, FROWS),)),
+        (pairs, pairs + 2, ()),
+    ):
+
+        @pl.loop(begin, end)
+        def _(step):
+            stages(step, row_sets)
 
     def last_pass(step, top):
         x = 2 * step
@@ -625,6 +661,30 @@
     finish_all(m_copies)
     for copy in blk_copies + slab_copies:
         copy.wait_send()
+
+
+def scale_kernel(in_hbm, scale_hbm, out_hbm, held, scale_ref, in_sems, out_sems, scale_sem):
+    chunks = [(c, pl.ds(h * (SIDE // 2), SIDE // 2)) for c in range(3) for h in range(2)]
+    fetch = [
+        pltpu.make_async_copy(in_hbm.at[chunk], held.at[chunk], in_sems.at[i])
+        for i, chunk in enumerate(chunks)
+    ]
+    store = [
+        pltpu.make_async_copy(held.at[chunk], out_hbm.at[chunk], out_sems.at[i])
+        for i, chunk in enumerate(chunks)
+    ]
+    fetch_scale = pltpu.make_async_copy(scale_hbm, scale_ref, scale_sem)
+    fetch_scale.start()
+    for copy in fetch:
+        copy.start()
+    fetch_scale.wait()
+    scale = scale_ref[...].reshape(1, 1, LANES)
+    for chunk, came, goes in zip(chunks, fetch, store):
+        came.wait()
+        held[chunk] = held[chunk] * scale
+        goes.start()
+    for goes in store:
+        goes.wait()
 
 
 def per_device(
@@ -713,7 +773,21 @@
         interp_level,
         block_mask,
     )
-    return smoothed * scale.reshape(1, 1, 1, LANES)
+    return pl.pallas_call(
+        scale_kernel,
+        out_shape=jax.ShapeDtypeStruct((3, SIDE, SIDE, LANES), F32),
+        in_specs=[pl.BlockSpec(memory_space=pltpu.HBM)] * 2,
+        out_specs=pl.BlockSpec(memory_space=pltpu.HBM),
+        scratch_shapes=[
+            pltpu.VMEM((3, SIDE, SIDE, LANES), F32),
+            pltpu.VMEM((1, LANES), F32),
+            sems(6),
+            sems(6),
+            pltpu.SemaphoreType.DMA,
+        ],
+        compiler_params=pltpu.CompilerParams(vmem_limit_bytes=64 * 1024 * 1024),
+        name="scale_step",
+    )(smoothed, scale)
 
 
 def solution(mesh):

time: 43.1 us -> 41.9 us (0.972)
  other arithmetic: 2.75 us -> 0 us
  Pallas kernels: 40.2 us -> 41.7 us
    mul x1 -> x0, other arithmetic: 2.75 us -> none  [per_device(): return smoothed * scale.reshape(1, 1, 1, LANES)]
    pallas_call x0 -> x1, Pallas kernels: none -> 2.41 us  [per_device(): pl.pallas_call(scale_kernel, out_shape=jax.ShapeDtypeStruct((3, SIDE, SID...]
    pallas_call x1, Pallas kernels: 40.2 us -> 39.3 us  [per_device(): pl.pallas_call(functools.partial(kernel, n_slab, n_blk), out_shape=(jax.S...]
where the time goes in v4:
time: 41.9 us; the launch traced here: 41.7 us
  Pallas kernels  41.7 us (100%)
    pallas_call x1, Pallas kernels, per_device(): pl.pallas_call(functools.partial(kernel, n_slab, n_blk), out_shape=(jax.S...  39.3 us
    pallas_call x1, Pallas kernels, per_device(): pl.pallas_call(scale_kernel, out_shape=jax.ShapeDtypeStruct((3, SIDE, SID...  2.41 us

profile of v4, /device:TPU:0, one launch (start us, length us, event | category | flops | bytes accessed | tf_op | source)
XLA Modules:
  0.0 41.7 jit_solution(13084748780275430884)
XLA Ops:
  0.0 39.3 %syn_step.1 = (f32[3,32,32,128]{3,2,1,0:T(8,128)}, f32[1,128]{1,0:T(1,128)}) custom-call(bf16[32,32,128]{2,1,0:T(8,128)(2,1)} %fixed_hbm.1, bf16[32,32,128]{2,1,0:T(8,128)(2,1)} %moving_hbm.1, s32[1,1,4,4]{3,2,1,0:T(4,128)} %owner_hbm.1, s32[1,1,4,4]{3,2,1,0:T(4,128)} %block_hbm.1, s32[1,1,4]{2,1,0:T(1,128)} %count_hbm.1, s32[1,1,3,4,4]{4,3,2,1,0:T(4,128)} %bitcast.1, ...), custom_call_target="tpu_custom_call" | custom-call | tf_op jit(solution)/shard_map/syn_step/pallas_call | solution.py:707
  39.3 2.4 %scale_step.1 = f32[3,32,32,128]{3,2,1,0:T(8,128)} custom-call(f32[3,32,32,128]{3,2,1,0:T(8,128)} %get-tuple-element.7.in_hbm, f32[1,128]{1,0:T(1,128)} %get-tuple-element.8.scale_hbm), custom_call_target="tpu_custom_call" | custom-call | tf_op jit(solution)/shard_map/scale_step/pallas_call | solution.py:776

commit v5 on v4

--- a/solution.py
+++ b/solution.py
@@ -79,8 +79,6 @@
     band_m,
     band_2,
     band_s,
-    fx_send,
-    fz_send,
     fx_recv,
     fz_recv,
     fc_recv,
@@ -192,7 +190,7 @@
                 ].astype(BF16)
                 x_send[side, j] = ext[HALO + at, FIRST : FIRST + SIDE, :].astype(BF16)
 
-    def fill_rims(copies, ext, x_recv, z_recv, c_recv, mask):
+    def fill_rims(copies, ext, x_recv, z_recv, c_recv):
         flat = ext.reshape(PLANES * ROWS, LANES)
         for i, (dx, dz) in enumerate(DIRECTIONS):
             at_x = 0 if dx > 0 else HALO + SIDE
@@ -216,14 +214,13 @@
                         rows = c_recv[i - 4, j].astype(F32)
                         rows = rows[16 - HALO :] if dx > 0 else rows[:HALO]
                         flat[pl.ds(at_x * ROWS + at_z + j, HALO, stride=ROWS), :] = rows
-                if mask:
-                    if dz == 0:
-                        plane = x_recv[side_x, HALO].astype(F32)
-                    elif dx == 0:
-                        plane = z_recv[side_z, HALO].astype(F32)
-                    else:
-                        plane = c_recv[i - 4, HALO].astype(F32)
-                    mask_pl[region, row_at : row_at + row_n, :] = plane[:row_n]
+                if dz == 0:
+                    plane = x_recv[side_x, HALO].astype(F32)
+                elif dx == 0:
+                    plane = z_recv[side_z, HALO].astype(F32)
+                else:
+                    plane = c_recv[i - 4, HALO].astype(F32)
+                mask_pl[region, row_at : row_at + row_n, :] = plane[:row_n]
 
     lane = lax.broadcasted_iota(jnp.int32, (1, LANES), 1)
 
@@ -233,35 +230,30 @@
             vec = jnp.where(lane // SIDE == g, scalars[g], vec)
         return vec
 
-    nought = me_b // n_blk
-    for ext in (f_ext, m_ext):
-
-        @pl.loop(0, PLANES // 7)
-        def _(x):
-            ext[pl.ds(x * 7, 7)] = jnp.zeros((7, ROWS, LANES), F32)
-
-    loads[0].wait()
-    loads[6].wait()
-
-    mask_pl[...] = jnp.zeros_like(mask_pl)
-    own_mask = by_block([mask_ref[0, 0, g] for g in range(4)]).astype(F32)
-    mask_rows = jnp.broadcast_to(own_mask, (SIDE, LANES))
-    mask_pl[1, SMOOTH_RADIUS : SMOOTH_RADIUS + SIDE, :] = mask_rows
-
-    @pl.loop(0, SIDE // 4)
-    def _(x):
-        at = pl.ds(HALO + x * 4, 4)
-        f_ext[at, FIRST : FIRST + SIDE, :] = fixed_ref[pl.ds(x * 4, 4)].astype(F32)
-
-    pack_rims(f_ext, fx_send, fz_send)
-    for side in range(2):
-        fx_send[side, HALO] = mask_rows.astype(BF16)
-        fz_send[side, HALO] = mask_rows.astype(BF16)
     wide_x = jnp.where(me_b > 0, 1, 0) + jnp.where(me_b < n_blk - 1, 1, 0)
     wide_z = jnp.where(me_s > 0, 1, 0) + jnp.where(me_s < n_slab - 1, 1, 0)
     pl.semaphore_wait(barrier, n_blk - 1 + n_slab - 1 + wide_x * wide_z)
 
-    f_copies = rim_copies(fx_send, fz_send, fx_recv, fz_recv, fc_recv, f_ssem, f_rsem)
+    f_copies = []
+    for i, (dx, dz) in enumerate(DIRECTIONS):
+        planes = pl.ds(0 if dx < 0 else SIDE - HALO, HALO)
+        rows = pl.ds(0 if dz < 0 else SIDE - 16, 16)
+        if dz == 0:
+            src, dst = fixed_hbm.at[planes], fx_recv.at[(dx + 1) // 2]
+        elif dx == 0:
+            src, dst = fixed_hbm.at[:, rows], fz_recv.at[(dz + 1) // 2]
+        else:
+            src, dst = fixed_hbm.at[planes, rows], fc_recv.at[i - 4]
+        f_copies.append(
+            pltpu.make_async_remote_copy(
+                src_ref=src,
+                dst_ref=dst,
+                send_sem=f_ssem.at[i],
+                recv_sem=f_rsem.at[i],
+                device_id=(me_s + dz, me_b + dx),
+                device_id_type=MESH,
+            )
+        )
     start_all(f_copies)
 
     if chips == 4:
@@ -319,6 +311,29 @@
             piece(3, h).start()
         passed(e, h).start()
 
+    nought = me_b // n_blk
+    for ext in (f_ext, m_ext):
+
+        @pl.loop(0, PLANES // 7)
+        def _(x):
+            ext[pl.ds(x * 7, 7)] = jnp.zeros((7, ROWS, LANES), F32)
+
+    loads[0].wait()
+    loads[6].wait()
+
+    mask_pl[...] = jnp.zeros_like(mask_pl)
+    own_mask = by_block([mask_ref[0, 0, g] for g in range(4)]).astype(F32)
+    mask_rows = jnp.broadcast_to(own_mask, (SIDE, LANES))
+    mask_pl[1, SMOOTH_RADIUS : SMOOTH_RADIUS + SIDE, :] = mask_rows
+
+    @pl.loop(0, SIDE // 4)
+    def _(x):
+        at = pl.ds(HALO + x * 4, 4)
+        f_ext[at, FIRST : FIRST + SIDE, :] = fixed_ref[pl.ds(x * 4, 4)].astype(F32)
+
+    for side in range(2):
+        mx_send[side, HALO] = mask_rows.astype(BF16)
+        mz_send[side, HALO] = mask_rows.astype(BF16)
     for load in loads[2:6]:
         load.wait()
     places, mixes = [], []
@@ -411,27 +426,40 @@
 
     per_box = 1.0 / float((2 * BOX_RADIUS + 1) ** 3)
 
-    def resample(e, begin=0, end=4):
-        @pl.loop(begin, end)
-        def _(part):
-            at = pl.ds(part * 8, 8)
-            pair = jnp.concatenate(
-                [gath[2 * e, at].reshape(256, LANES), gath[2 * e + 1, at].reshape(256, LANES)],
-                axis=1,
-            )
-            pair = jnp.concatenate([pair, pair], axis=1)
-            got = jnp.dot(pair, select[e], preferred_element_type=F32)
-            rows = pl.ds(part * 256, 256)
-            if e == 0:
-                acc[rows, :] = got
-            else:
-                acc[rows, :] = acc[rows, :] + got
+    def resample(first_e, last_e, h):
+        at = slice(h * half, (h + 1) * half)
+        rows = slice(h * half * SIDE, (h + 1) * half * SIDE)
+        blocks = []
+        for e in range(first_e, last_e):
+            pair = [gath[2 * e + p, at].reshape(half * SIDE, LANES) for p in range(2)]
+            blocks += pair + pair
+        got = jnp.dot(
+            jnp.concatenate(blocks, axis=1),
+            select[first_e:last_e].reshape((last_e - first_e) * 4 * LANES, 4 * LANES),
+            preferred_element_type=F32,
+        )
+        acc[rows, :] = got if first_e == 0 else acc[rows, :] + got
 
     if chips == 4:
         take(1, 0)
         take(2, 1)
 
-    fill_rims(f_copies, f_ext, fx_recv, fz_recv, fc_recv, True)
+    for i, (dx, dz) in enumerate(DIRECTIONS):
+        planes = {1: slice(0, HALO), 0: slice(HALO, HALO + SIDE), -1: slice(HALO + SIDE, PLANES)}[dx]
+
+        @pl.when(there(-dx, -dz))
+        def _():
+            f_copies[i].wait_recv()
+            if dz == 0:
+                f_ext[planes, FIRST : FIRST + SIDE] = fx_recv[(dx + 1) // 2].astype(F32)
+            else:
+                slab = fz_recv[(dz + 1) // 2] if dx == 0 else fc_recv[i - 4]
+                slab = slab.astype(F32)
+                if dz > 0:
+                    f_ext[planes, :FIRST] = slab[:, 8:]
+                else:
+                    f_ext[planes, FIRST + SIDE :] = slab[:, :8]
+
 
     @pl.loop(0, PLANES // 7)
     def _(step):
@@ -451,11 +479,6 @@
         for j in range(2):
             for q in range(2):
                 z_sum(q, 2 * step + j)
-
-    loads[1].wait()
-    for h in range(2):
-        passed(0, h).wait_recv()
-    resample(0)
 
     @pl.loop(0, FPLANES // 2)
     def _(step):
@@ -472,15 +495,17 @@
         for e in range(1, chips):
             for h in range(2):
                 take(e, h)
-    for e in range(1, chips):
+    loads[1].wait()
+    for e in range(chips - 1):
         for h in range(2):
-            if chips == 4 and e == 2:
-                take(3, h)
             passed(e, h).wait_recv()
-            if e == chips - 1:
-                resample(e, 2 * h, 2 * h + 2)
-        if e < chips - 1:
-            resample(e)
+    for h in range(2):
+        resample(0, chips - 1, h)
+        if chips == 4:
+            take(3, h)
+    for h in range(2):
+        passed(chips - 1, h).wait_recv()
+        resample(chips - 1, chips, h)
 
     last_row = lax.broadcasted_iota(jnp.int32, (SIDE, LANES), 0) == SIDE - 1
 
@@ -555,7 +580,7 @@
     def _(now):
         force_rows(now, inner)
 
-    fill_rims(m_copies, m_ext, mx_recv, mz_recv, mc_recv, False)
+    fill_rims(m_copies, m_ext, mx_recv, mz_recv, mc_recv)
     y_pass(slice(0, HALO), slice(None), (HALO, ROWS))
     y_pass(slice(HALO + SIDE, PLANES), slice(None), (HALO, ROWS))
     y_pass(slice(HALO, HALO + SIDE), slice(0, FIRST), (SIDE, FIRST))
@@ -736,16 +761,14 @@
             pltpu.VMEM((LANES, 2 * LANES), BF16),
             pltpu.VMEM((2 * LANES, LANES), BF16),
             pltpu.VMEM((LANES, 2 * LANES), BF16),
+            rim(HALO, SIDE, 2),
+            rim(SIDE, 16, 2),
+            rim(HALO, 16, 4),
             rim(HALO + 1, SIDE, 2),
             rim(HALO + 1, SIDE, 2),
             rim(HALO + 1, SIDE, 2),
             rim(HALO + 1, SIDE, 2),
             rim(HALO + 1, 16, 4),
-            rim(HALO, SIDE, 2),
-            rim(HALO, SIDE, 2),
-            rim(HALO, SIDE, 2),
-            rim(HALO, SIDE, 2),
-            rim(HALO, 16, 4),
             pltpu.VMEM((2, 8, LANES), F32),
             pltpu.VMEM((n_blk, 8, LANES), F32),
             pltpu.VMEM((n_slab, 8, LANES), F32),

time: 41.9 us -> 41.1 us (0.981)
  Pallas kernels: 41.7 us -> 41 us
    pallas_call x1, Pallas kernels: 39.3 us -> 38.5 us  [per_device(): pl.pallas_call(functools.partial(kernel, n_slab, n_blk), out_shape=(jax.S...]
where the time goes in v5:
time: 41.1 us; the launch traced here: 41 us
  Pallas kernels  41 us (100%)
    pallas_call x1, Pallas kernels, per_device(): pl.pallas_call(functools.partial(kernel, n_slab, n_blk), out_shape=(jax.S...  38.5 us
    pallas_call x1, Pallas kernels, per_device(): pl.pallas_call(scale_kernel, out_shape=jax.ShapeDtypeStruct((3, SIDE, SID...  2.41 us

profile of v5, /device:TPU:0, one launch (start us, length us, event | category | flops | bytes accessed | tf_op | source)
XLA Modules:
  0.0 41.0 jit_solution(11138953354606218677)
XLA Ops:
  0.0 38.5 %syn_step.1 = (f32[3,32,32,128]{3,2,1,0:T(8,128)}, f32[1,128]{1,0:T(1,128)}) custom-call(bf16[32,32,128]{2,1,0:T(8,128)(2,1)} %fixed_hbm.1, bf16[32,32,128]{2,1,0:T(8,128)(2,1)} %moving_hbm.1, s32[1,1,4,4]{3,2,1,0:T(4,128)} %owner_hbm.1, s32[1,1,4,4]{3,2,1,0:T(4,128)} %block_hbm.1, s32[1,1,4]{2,1,0:T(1,128)} %count_hbm.1, s32[1,1,3,4,4]{4,3,2,1,0:T(4,128)} %bitcast.1, ...), custom_call_target="tpu_custom_call" | custom-call | tf_op jit(solution)/shard_map/syn_step/pallas_call | solution.py:732
  38.6 2.4 %scale_step.1 = f32[3,32,32,128]{3,2,1,0:T(8,128)} custom-call(f32[3,32,32,128]{3,2,1,0:T(8,128)} %get-tuple-element.7.in_hbm, f32[1,128]{1,0:T(1,128)} %get-tuple-element.8.scale_hbm), custom_call_target="tpu_custom_call" | custom-call | tf_op jit(solution)/shard_map/scale_step/pallas_call | solution.py:799

commit v6 on v5

--- a/solution.py
+++ b/solution.py
@@ -79,6 +79,7 @@
     band_m,
     band_2,
     band_s,
+    band_z,
     fx_recv,
     fz_recv,
     fc_recv,
@@ -399,8 +400,21 @@
     for t in range(2 * SMOOTH_RADIUS + 1):
         bell = jnp.where(off == t - SMOOTH_RADIUS, taps[t], bell)
     bell_hi = bell.astype(BF16)
-    band_s[:, :LANES] = bell_hi
-    band_s[:, LANES:] = (bell - bell_hi.astype(F32)).astype(BF16)
+    for part in range(2):
+        rows = slice(part * LANES, (part + 1) * LANES)
+        band_s[rows, :LANES] = bell_hi
+        band_s[rows, LANES:] = (bell - bell_hi.astype(F32)).astype(BF16)
+    ahead = lax.broadcasted_iota(jnp.int32, (SIDE, 2 * LANES), 1) - lax.broadcasted_iota(
+        jnp.int32, (SIDE, 2 * LANES), 0
+    )
+    for b in range(6):
+        bell = jnp.zeros((SIDE, 2 * LANES), F32)
+        for t in range(2 * SMOOTH_RADIUS + 1):
+            bell = jnp.where(ahead == FROWS * b + t, taps[t], bell)
+        bell_hi = bell.astype(BF16)
+        band_z[SIDE * b : SIDE * (b + 1)] = bell_hi
+        band_z[SIDE * (6 + b) : SIDE * (7 + b)] = (bell - bell_hi.astype(F32)).astype(BF16)
+    forces[:, 6 * FROWS :] = jnp.zeros((FPLANES // 2, 2 * LANES - 6 * FROWS, LANES), F32)
 
     def halves(product):
         high = product.astype(BF16)
@@ -607,14 +621,14 @@
 
     def stages(step, row_sets):
         old = jnp.maximum(step - 2, 0)
+        both = jnp.dot(halves(ysm[old]), band_s[...], preferred_element_type=F32)
+        both = (both[:, :LANES] + both[:, LANES:]).reshape(6, SIDE, LANES)
         for j in range(2):
             for c in range(3):
-                zsm[c, 2 * old + j] = bell_sum(
-                    [shifted(ysm, (old, 3 * j + c), t, SIDE) for t in range(7)]
-                )
+                zsm[c, 2 * old + j] = both[3 * j + c]
         mid = jnp.minimum(jnp.maximum(step - 1, 0), pairs - 1)
-        both = jnp.dot(forces[mid].astype(BF16), band_s[...], preferred_element_type=F32)
-        ysm[mid] = (both[:, :LANES] + both[:, LANES:]).reshape(6, FROWS, LANES)
+        both = jnp.dot(band_z[...], forces[mid].astype(BF16), preferred_element_type=F32)
+        ysm[mid] = both[: 6 * SIDE] + both[6 * SIDE :]
         for rows in row_sets:
             force_rows(step, rows)
 
@@ -754,13 +768,14 @@
             pltpu.VMEM((FPLANES, FROWS, LANES), F32),
             pltpu.VMEM((FPLANES, FROWS, LANES), F32),
             pltpu.VMEM((PLANES, ROWS, LANES), F32),
-            pltpu.VMEM((FPLANES // 2, 6 * FROWS, LANES), F32),
-            pltpu.VMEM((FPLANES // 2, 6, FROWS, LANES), F32),
+            pltpu.VMEM((FPLANES // 2, 2 * LANES, LANES), F32),
+            pltpu.VMEM((FPLANES // 2, 6 * SIDE, LANES), F32),
             pltpu.VMEM((3, FPLANES, SIDE, LANES), F32),
             pltpu.VMEM((3, FROWS, LANES), F32),
             pltpu.VMEM((LANES, 2 * LANES), BF16),
             pltpu.VMEM((2 * LANES, LANES), BF16),
-            pltpu.VMEM((LANES, 2 * LANES), BF16),
+            pltpu.VMEM((2 * LANES, 2 * LANES), BF16),
+            pltpu.VMEM((12 * SIDE, 2 * LANES), BF16),
             rim(HALO, SIDE, 2),
             rim(SIDE, 16, 2),
             rim(HALO, 16, 4),

time: 41.1 us -> 42 us (1.022)
  Pallas kernels: 41 us -> 41.9 us
    pallas_call x1, Pallas kernels: 38.5 us -> 39.4 us  [per_device(): pl.pallas_call(functools.partial(kernel, n_slab, n_blk), out_shape=(jax.S...]
where the time goes in v6:
time: 42 us; the launch traced here: 41.9 us
  Pallas kernels  41.9 us (100%)
    pallas_call x1, Pallas kernels, per_device(): pl.pallas_call(functools.partial(kernel, n_slab, n_blk), out_shape=(jax.S...  39.4 us
    pallas_call x1, Pallas kernels, per_device(): pl.pallas_call(scale_kernel, out_shape=jax.ShapeDtypeStruct((3, SIDE, SID...  2.41 us

profile of v6, /device:TPU:0, one launch (start us, length us, event | category | flops | bytes accessed | tf_op | source)
XLA Modules:
  0.0 41.9 jit_solution(14011450173117674917)
XLA Ops:
  0.0 39.4 %syn_step.1 = (f32[3,32,32,128]{3,2,1,0:T(8,128)}, f32[1,128]{1,0:T(1,128)}) custom-call(bf16[32,32,128]{2,1,0:T(8,128)(2,1)} %fixed_hbm.1, bf16[32,32,128]{2,1,0:T(8,128)(2,1)} %moving_hbm.1, s32[1,1,4,4]{3,2,1,0:T(4,128)} %owner_hbm.1, s32[1,1,4,4]{3,2,1,0:T(4,128)} %block_hbm.1, s32[1,1,4]{2,1,0:T(1,128)} %count_hbm.1, s32[1,1,3,4,4]{4,3,2,1,0:T(4,128)} %bitcast.1, ...), custom_call_target="tpu_custom_call" | custom-call | tf_op jit(solution)/shard_map/syn_step/pallas_call | solution.py:746
  39.5 2.4 %scale_step.1 = f32[3,32,32,128]{3,2,1,0:T(8,128)} custom-call(f32[3,32,32,128]{3,2,1,0:T(8,128)} %get-tuple-element.7.in_hbm, f32[1,128]{1,0:T(1,128)} %get-tuple-element.8.scale_hbm), custom_call_target="tpu_custom_call" | custom-call | tf_op jit(solution)/shard_map/scale_step/pallas_call | solution.py:814

commit v7 on v5

--- a/solution.py
+++ b/solution.py
@@ -576,9 +576,11 @@
 
     pairs = FPLANES // 2
 
-    @pl.loop(edge, pairs - edge)
+    @pl.loop(edge, pairs - edge - 1, unroll=2)
     def _(now):
         force_rows(now, inner)
+
+    force_rows(pairs - edge - 1, inner)
 
     fill_rims(m_copies, m_ext, mx_recv, mz_recv, mc_recv)
     y_pass(slice(0, HALO), slice(None), (HALO, ROWS))
@@ -618,14 +620,15 @@
         for rows in row_sets:
             force_rows(step, rows)
 
-    for begin, end, row_sets in (
-        (0, edge, (slice(0, FROWS),)),
-        (edge, pairs - edge, outer),
-        (pairs - edge, pairs, (slice(0, FROWS),)),
-        (pairs, pairs + 2, ()),
+    for begin, end, unroll, row_sets in (
+        (0, edge, edge, (slice(0, FROWS),)),
+        (edge, pairs - edge - 1, 4, outer),
+        (pairs - edge - 1, pairs - edge, 1, outer),
+        (pairs - edge, pairs, edge, (slice(0, FROWS),)),
+        (pairs, pairs + 2, 2, ()),
     ):
 
-        @pl.loop(begin, end)
+        @pl.loop(begin, end, unroll=unroll)
         def _(step):
             stages(step, row_sets)
 
@@ -640,7 +643,9 @@
                 squares[j] = squares[j] + value * value
         return jnp.maximum(top, jnp.maximum(squares[0], squares[1]))
 
-    top = lax.fori_loop(0, SIDE // 2, last_pass, jnp.zeros((SIDE, LANES), F32))
+    top = lax.fori_loop(
+        0, SIDE // 2, last_pass, jnp.zeros((SIDE, LANES), F32), unroll=2
+    )
     top = jnp.max(top.reshape(4, 8, LANES), axis=0)
     write = pltpu.make_async_copy(out_ref, out_hbm, out_sem)
     write.start()

time: 41.1 us -> 38.8 us (0.944)
  Pallas kernels: 41 us -> 38.6 us
    pallas_call x1, Pallas kernels: 38.5 us -> 36.2 us  [per_device(): pl.pallas_call(functools.partial(kernel, n_slab, n_blk), out_shape=(jax.S...]
where the time goes in v7:
time: 38.8 us; the launch traced here: 38.6 us
  Pallas kernels  38.6 us (99%)
    pallas_call x1, Pallas kernels, per_device(): pl.pallas_call(functools.partial(kernel, n_slab, n_blk), out_shape=(jax.S...  36.2 us
    pallas_call x1, Pallas kernels, per_device(): pl.pallas_call(scale_kernel, out_shape=jax.ShapeDtypeStruct((3, SIDE, SID...  2.41 us

profile of v7, /device:TPU:0, one launch (start us, length us, event | category | flops | bytes accessed | tf_op | source)
XLA Modules:
  0.0 38.6 jit_solution(3641144322907998242)
XLA Ops:
  0.0 36.2 %syn_step.1 = (f32[3,32,32,128]{3,2,1,0:T(8,128)}, f32[1,128]{1,0:T(1,128)}) custom-call(bf16[32,32,128]{2,1,0:T(8,128)(2,1)} %fixed_hbm.1, bf16[32,32,128]{2,1,0:T(8,128)(2,1)} %moving_hbm.1, s32[1,1,4,4]{3,2,1,0:T(4,128)} %owner_hbm.1, s32[1,1,4,4]{3,2,1,0:T(4,128)} %block_hbm.1, s32[1,1,4]{2,1,0:T(1,128)} %count_hbm.1, s32[1,1,3,4,4]{4,3,2,1,0:T(4,128)} %bitcast.1, ...), custom_call_target="tpu_custom_call" | custom-call | tf_op jit(solution)/shard_map/syn_step/pallas_call | solution.py:737
  36.2 2.4 %scale_step.1 = f32[3,32,32,128]{3,2,1,0:T(8,128)} custom-call(f32[3,32,32,128]{3,2,1,0:T(8,128)} %get-tuple-element.7.in_hbm, f32[1,128]{1,0:T(1,128)} %get-tuple-element.8.scale_hbm), custom_call_target="tpu_custom_call" | custom-call | tf_op jit(solution)/shard_map/scale_step/pallas_call | solution.py:804
